TPU v7x, 32 devices: a whole 2x2x4 slice. The times are simulated.
32 devices in a mesh: gx: 4 (over y, x), gy: 4 (over z), dst: 2 (over core).
Axes of the slice: x: 2, y: 2, z: 4, core: 2. Of those that a mesh axis runs over, the one named last changes fastest.
Arguments:
- features: bfloat16 [32, 8, 16384], P(None, None, ('gx', 'gy')), may hold values from 0.09 to 3.1
- cost_weights: float32 [32], replicated, may hold values from 0.1 to 1
- successors: int32 [8, 16384], P(None, ('gx', 'gy')), may hold values from 0 to 1535, as said below
- turn_valid: int32 [8, 16384], P(None, ('gx', 'gy')), may hold values from 0 to 1, as said below
- border_lists: int32 [4, 2048], P(None, ('gx', 'gy')), may hold values from 0 to 1023, as said below
- destinations: int32 [32], P('dst'), may hold values from 0 to 16383
- anchors: float32 [32, 16384], P('dst', ('gx', 'gy')), may hold values from 0.25 to 4
- demo_counts: int32 [8, 16384], P(None, ('gx', 'gy')), may hold values from 0 to 3
Outputs:
- count_gap: float32 [8, 16384], P(None, ('gx', 'gy'))
- gradient: float32 [32], replicated
Inputs may be any that keep to these rules, and one draw needn't show every extreme that they name: `successors`: values below 1024 are segments of the same block and turn 0 is always one of them; 1024 + k * 128 + j is entry j of the border list of the neighbour on side k (0: one gx position lower, 1: higher, 2: one gy position lower, 3: higher) that faces this block. `turn_valid`: turn 0 is always 1; a turn into a side where the grid has no neighbouring block is 0. `border_lists`: within one block and side the 128 entries are distinct local segment numbers.
All inputs are finite; a program needn't handle non-finite values.
Results may differ from a plain program's by a relative error of at most 0.0003.
Values sent between devices are 32-bit elements; how exact they have to be, the bound alone decides.
No kernel may reach another device: no remote copies, remote signals or barrier semaphores. Data moves between devices by JAX's collectives and lax.ppermute only.
A program may use at most 64 MiB of HBM per device.

v0:
```python
import jax
import jax.numpy as jnp
from jax import lax
from jax.sharding import PartitionSpec as P

HORIZON = 8


NEG = -1e30
START_COST = 100.0


def passed_along(array, axis, by):
    length = lax.axis_size(axis)
    pairs = [(i, i + by) for i in range(length) if 0 <= i + by < length]
    return lax.ppermute(array, axis, pairs)


def bring_values(values, border_lists):
    outgoing = values[:, border_lists]
    north_part = passed_along(outgoing[:, 1], "gx", 1)
    south_part = passed_along(outgoing[:, 0], "gx", -1)
    west_part = passed_along(outgoing[:, 3], "gy", 1)
    east_part = passed_along(outgoing[:, 2], "gy", -1)
    return jnp.concatenate([north_part, south_part, west_part, east_part], axis=1)


def return_flow(arrived, border_lists, own_count, border_width):
    local_part = arrived[:, :own_count]
    halo_part = arrived[:, own_count:].reshape(arrived.shape[0], 4, border_width)
    from_south = passed_along(halo_part[:, 0], "gx", -1)
    from_north = passed_along(halo_part[:, 1], "gx", 1)
    from_east = passed_along(halo_part[:, 2], "gy", -1)
    from_west = passed_along(halo_part[:, 3], "gy", 1)
    returned = jnp.stack([from_north, from_south, from_west, from_east], axis=1)
    return local_part.at[:, border_lists].add(returned)


def select_cells(cells, flat_index, turn_shape):
    picked = jnp.take(cells, flat_index, axis=1)
    return picked.reshape(cells.shape[0], turn_shape[0], turn_shape[1])


def turn_scores(values, halo_cells, reward, flat_turns, usable):
    extended = jnp.concatenate([values, halo_cells], axis=1)
    scores = reward[None] + select_cells(extended, flat_turns, usable.shape)
    return jnp.where(usable[None], scores, NEG)


def local(
    features, cost_weights, successors, turn_valid, border_lists, destinations, anchors, demo_counts
):
    own_count = successors.shape[1]
    border_width = border_lists.shape[1]
    dest_count = anchors.shape[0]
    slot_total = own_count + 4 * border_width
    block_index = lax.axis_index("gx") * lax.axis_size("gy") + lax.axis_index("gy")
    positions = jnp.arange(own_count, dtype=jnp.int32)
    is_target = positions[None, :] == (destinations - block_index * own_count)[:, None]
    usable = turn_valid == 1
    feats = features.astype(jnp.float32)
    reward = -jnp.sum(feats * cost_weights[:, None, None], axis=0)
    flat_turns = successors.reshape(-1)
    values = jnp.where(is_target, 0.0, -START_COST).astype(jnp.float32)
    for round_index in range(HORIZON):
        halo_cells = bring_values(values, border_lists)
        scores = turn_scores(values, halo_cells, reward, flat_turns, usable)
        row_max = jnp.max(scores, axis=1)
        new_values = row_max + jnp.log(jnp.sum(jnp.exp(scores - row_max[:, None]), axis=1))
        values = jnp.where(is_target, 0.0, new_values)
    halo_cells = bring_values(values, border_lists)
    scores = turn_scores(values, halo_cells, reward, flat_turns, usable)
    row_max = jnp.max(scores, axis=1)
    raised = jnp.exp(scores - row_max[:, None])
    policy = raised / jnp.sum(raised, axis=1, keepdims=True)
    mass_now = jnp.where(is_target, 0.0, anchors)
    turn_counts = jnp.zeros(successors.shape, jnp.float32)
    for round_index in range(HORIZON):
        turn_flow = mass_now[:, None, :] * policy
        turn_counts = turn_counts + jnp.sum(turn_flow, axis=0)
        if round_index + 1 < HORIZON:
            arrived = (
                jnp.zeros((dest_count, slot_total), jnp.float32)
                .at[:, flat_turns]
                .add(turn_flow.reshape(dest_count, -1))
            )
            landed = return_flow(arrived, border_lists, own_count, border_width)
            mass_now = jnp.where(is_target, 0.0, landed)
    local_visits = turn_counts / (dest_count * lax.axis_size("dst") * HORIZON)
    visits = lax.psum(local_visits, "dst")
    demo_term = jnp.where(usable, demo_counts, 0).astype(jnp.float32) / 3.0
    count_gap = demo_term - visits
    total_segments = own_count * lax.axis_size("gx") * lax.axis_size("gy")
    own_gap = demo_term / lax.axis_size("dst") - local_visits
    block_term = jnp.sum(own_gap[None] * feats, axis=(1, 2)) / total_segments
    gradient = lax.psum(block_term, ("gx", "gy", "dst"))
    return (count_gap, gradient)


def solution(mesh):
    in_specs = (
        P(None, None, ("gx", "gy")),
        P(),
        P(None, ("gx", "gy")),
        P(None, ("gx", "gy")),
        P(None, ("gx", "gy")),
        P("dst"),
        P("dst", ("gx", "gy")),
        P(None, ("gx", "gy")),
    )
    out_specs = (P(None, ("gx", "gy")), P())
    return jax.shard_map(local, mesh=mesh, in_specs=in_specs, out_specs=out_specs, check_vma=False)
```

profile of v0, /device:TPU:0, one launch (start us, length us, event | category | flops | bytes accessed | tf_op | source)
XLA Modules:
  0.0 1007.5 jit_solution(16982263539445634157)
XLA Ops:
  18.9 27.7 %gather_fusion.9 = f32[8192,16]{1,0:T(8,128)} fusion(f32[16,1536]{0,1:T(8,128)S(1)} %constant_dynamic-update-slice_fusion, s32[8192]{0:T(1024)S(1)} %fusion.45), kind=kCustom, calls=%fused_computation.clone | custom fusion | bytes 1081344 | tf_op jit(solution)/shard_map/jit(_take)/gather | solution.py:40
  46.6 6.2 broadcast_select_fusion.8
  75.2 27.7 %gather_fusion.10 = f32[8192,16]{1,0:T(8,128)} fusion(f32[16,1536]{0,1:T(8,128)S(1)} %constant_dynamic-update-slice_fusion.4, s32[8192]{0:T(1024)S(1)} %fusion.45), kind=kCustom, calls=%fused_computation.1.clone | custom fusion | bytes 1081344 | tf_op jit(solution)/shard_map/jit(_take)/gather | solution.py:40
  102.9 6.2 broadcast_select_fusion.7
  131.9 27.7 %gather_fusion.11 = f32[8192,16]{1,0:T(8,128)} fusion(f32[16,1536]{0,1:T(8,128)S(1)} %constant_dynamic-update-slice_fusion.9, s32[8192]{0:T(1024)S(1)} %fusion.45), kind=kCustom, calls=%fused_computation.2.clone | custom fusion | bytes 1081344 | tf_op jit(solution)/shard_map/jit(_take)/gather | solution.py:40
  159.6 6.2 broadcast_select_fusion.6
  188.9 27.7 %gather_fusion.12 = f32[8192,16]{1,0:T(8,128)} fusion(f32[16,1536]{0,1:T(8,128)S(1)} %constant_dynamic-update-slice_fusion.14, s32[8192]{0:T(1024)S(1)} %fusion.45), kind=kCustom, calls=%fused_computation.3.clone | custom fusion | bytes 1081344 | tf_op jit(solution)/shard_map/jit(_take)/gather | solution.py:40
  216.6 6.2 broadcast_select_fusion.5
  244.5 27.7 %gather_fusion.13 = f32[8192,16]{1,0:T(8,128)} fusion(f32[16,1536]{0,1:T(8,128)S(1)} %constant_dynamic-update-slice_fusion.19, s32[8192]{0:T(1024)S(1)} %fusion.45), kind=kCustom, calls=%fused_computation.4.clone | custom fusion | bytes 1081344 | tf_op jit(solution)/shard_map/jit(_take)/gather | solution.py:40
  272.2 6.2 broadcast_select_fusion.4
  300.4 27.7 %gather_fusion.14 = f32[8192,16]{1,0:T(8,128)} fusion(f32[16,1536]{0,1:T(8,128)S(1)} %constant_dynamic-update-slice_fusion.24, s32[8192]{0:T(1024)S(1)} %fusion.45), kind=kCustom, calls=%fused_computation.5.clone | custom fusion | bytes 1081344 | tf_op jit(solution)/shard_map/jit(_take)/gather | solution.py:40
  328.0 6.2 broadcast_select_fusion.3
  356.0 27.7 %gather_fusion.15 = f32[8192,16]{1,0:T(8,128)} fusion(f32[16,1536]{0,1:T(8,128)S(1)} %constant_dynamic-update-slice_fusion.29, s32[8192]{0:T(1024)S(1)} %fusion.45), kind=kCustom, calls=%fused_computation.6.clone | custom fusion | bytes 1081344 | tf_op jit(solution)/shard_map/jit(_take)/gather | solution.py:40
  383.7 6.2 broadcast_select_fusion.2
  411.9 27.7 %gather_fusion.16 = f32[8192,16]{1,0:T(8,128)} fusion(f32[16,1536]{0,1:T(8,128)S(1)} %constant_dynamic-update-slice_fusion.34, s32[8192]{0:T(1024)S(1)} %fusion.45), kind=kCustom, calls=%fused_computation.7.clone | custom fusion | bytes 1081344 | tf_op jit(solution)/shard_map/jit(_take)/gather | solution.py:40
  439.6 6.2 broadcast_select_fusion.1
  467.6 27.7 %gather_fusion.17 = f32[8192,16]{1,0:T(8,128)} fusion(f32[16,1536]{0,1:T(8,128)S(1)} %constant_dynamic-update-slice_fusion.39, s32[8192]{0:T(1024)S(1)} %fusion.45), kind=kCustom, calls=%fused_computation.8.clone | custom fusion | bytes 1081344 | tf_op jit(solution)/shard_map/jit(_take)/gather | solution.py:40
  495.3 6.2 broadcast_select_fusion
  507.2 6.0 fusion.48
  513.3 41.0 %scatter_custom_fusion = f32[16,1536]{0,1:T(8,128)S(1)} fusion(s32[8192]{0:T(1024)S(1)} %bitcast.343, f32[16,8192]{0,1:T(8,128)} %get-tuple-element.6, f32[]{:T(128)} %constant.17.clone.1), kind=kCustom, calls=%fused_computation.52 | custom fusion | flops 131072 | bytes 622596 | tf_op jit(solution)/shard_map/scatter-add | solution.py:85
  561.7 6.1 collective-permute-start.36
  578.0 40.5 %scatter_custom_fusion.2 = f32[16,1536]{0,1:T(8,128)S(1)} fusion(s32[8192]{0:T(1024)S(1)} %bitcast.344, f32[16,8192]{0,1:T(8,128)} %get-tuple-element.4, f32[]{:T(128)} %constant.17.clone.1), kind=kCustom, calls=%fused_computation.49 | custom fusion | flops 131072 | bytes 622596 | tf_op jit(solution)/shard_map/scatter-add | solution.py:85
  641.8 40.7 %scatter_custom_fusion.4 = f32[16,1536]{0,1:T(8,128)S(1)} fusion(s32[8192]{0:T(1024)S(1)} %bitcast.345, f32[16,8192]{0,1:T(8,128)} %get-tuple-element.9, f32[]{:T(128)} %constant.17.clone.1), kind=kCustom, calls=%fused_computation.46 | custom fusion | flops 131072 | bytes 622596 | tf_op jit(solution)/shard_map/scatter-add | solution.py:85
  689.9 5.7 collective-permute-start.44
  705.9 40.5 %scatter_custom_fusion.6 = f32[16,1536]{0,1:T(8,128)S(1)} fusion(s32[8192]{0:T(1024)S(1)} %bitcast.346, f32[16,8192]{0,1:T(8,128)} %get-tuple-element.11, f32[]{:T(128)} %constant.17.clone.1), kind=kCustom, calls=%fused_computation.43 | custom fusion | flops 131072 | bytes 622596 | tf_op jit(solution)/shard_map/scatter-add | solution.py:85
  753.9 5.7 collective-permute-start.48
  770.0 40.8 %scatter_custom_fusion.8 = f32[16,1536]{0,1:T(8,128)S(1)} fusion(s32[8192]{0:T(1024)S(1)} %bitcast.347, f32[16,8192]{0,1:T(8,128)} %get-tuple-element.13, f32[]{:T(128)} %constant.17.clone.1), kind=kCustom, calls=%fused_computation.40 | custom fusion | flops 131072 | bytes 622596 | tf_op jit(solution)/shard_map/scatter-add | solution.py:85
  818.2 5.7 collective-permute-start.52
  834.2 40.5 %scatter_custom_fusion.10 = f32[16,1536]{0,1:T(8,128)S(1)} fusion(s32[8192]{0:T(1024)S(1)} %bitcast.348, f32[16,8192]{0,1:T(8,128)} %get-tuple-element.15, f32[]{:T(128)} %constant.17.clone.1), kind=kCustom, calls=%fused_computation.37 | custom fusion | flops 131072 | bytes 622596 | tf_op jit(solution)/shard_map/scatter-add | solution.py:85
  898.2 40.8 %scatter_custom_fusion.12 = f32[16,1536]{0,1:T(8,128)S(1)} fusion(s32[8192]{0:T(1024)S(1)} %bitcast.349, f32[16,8192]{0,1:T(8,128)} %get-tuple-element.17, f32[]{:T(128)} %constant.17.clone.1), kind=kCustom, calls=%fused_computation.34 | custom fusion | flops 131072 | bytes 622596 | tf_op jit(solution)/shard_map/scatter-add | solution.py:85
  946.6 5.9 collective-permute-start.60
  965.3 41.7 %psum.15 = f32[32]{0:T(128)} all-reduce(f32[32]{0:T(128)S(1)} %broadcast_multiply_fusion), channel_id=1, replica_groups=mesh['gx'=4,'gy'=4,'dst'=2] {'gx','gy','dst'}, use_global_device_ids=true, to_apply=%region_43.45 | all-reduce | flops 32 | bytes 256 | tf_op jit(solution)/shard_map/psum | solution.py:96
  (320 shorter events, 337.5 us)
Async XLA Ops:
  3.1 14.5 %collective-permute-start = (f32[16,128]{0,1:T(8,128)S(1)}, f32[16,128]{0,1:T(8,128)S(1)}, u32[]{:S(2)}, u32[]{:S(2)}) collective-permute-start(f32[16,128]{0,1:T(8,128)S(1)} %get-tuple-element.97), channel_id=1, source_target_pairs={{0,8},{8,16},{16,24},{1,9},{9,17},{17,25},{2,10},{10,18},{18,26},{... | collective-permute-start | bytes 24584 | tf_op jit(solution)/shard_map/ppermute | solution.py:16
  8.0 9.7 collective-permute-start.1
  9.3 8.4 collective-permute-start.2
  59.7 10.7 %collective-permute-start.4 = (f32[16,128]{0,1:T(8,128)S(1)}, f32[16,128]{0,1:T(8,128)S(1)}, u32[]{:S(2)}, u32[]{:S(2)}) collective-permute-start(f32[16,128]{0,1:T(8,128)S(1)} %get-tuple-element.93), channel_id=1, source_target_pairs={{0,8},{8,16},{16,24},{1,9},{9,17},{17,25},{2,10},{10,18},{18,26},{... | collective-permute-start | bytes 24584 | tf_op jit(solution)/shard_map/ppermute | solution.py:16
  116.0 11.0 %collective-permute-start.8 = (f32[16,128]{0,1:T(8,128)S(1)}, f32[16,128]{0,1:T(8,128)S(1)}, u32[]{:S(2)}, u32[]{:S(2)}) collective-permute-start(f32[16,128]{0,1:T(8,128)S(1)} %get-tuple-element.89), channel_id=1, source_target_pairs={{0,8},{8,16},{16,24},{1,9},{9,17},{17,25},{2,10},{10,18},{18,26},{... | collective-permute-start | bytes 24584 | tf_op jit(solution)/shard_map/ppermute | solution.py:16
  172.6 11.4 %collective-permute-start.12 = (f32[16,128]{0,1:T(8,128)S(1)}, f32[16,128]{0,1:T(8,128)S(1)}, u32[]{:S(2)}, u32[]{:S(2)}) collective-permute-start(f32[16,128]{0,1:T(8,128)S(1)} %get-tuple-element.85), channel_id=1, source_target_pairs={{0,8},{8,16},{16,24},{1,9},{9,17},{17,25},{2,10},{10,18},{18,26},{... | collective-permute-start | bytes 24584 | tf_op jit(solution)/shard_map/ppermute | solution.py:16
  229.7 10.0 collective-permute-start.16
  285.3 10.2 %collective-permute-start.20 = (f32[16,128]{0,1:T(8,128)S(1)}, f32[16,128]{0,1:T(8,128)S(1)}, u32[]{:S(2)}, u32[]{:S(2)}) collective-permute-start(f32[16,128]{0,1:T(8,128)S(1)} %get-tuple-element.77), channel_id=1, source_target_pairs={{0,8},{8,16},{16,24},{1,9},{9,17},{17,25},{2,10},{10,18},{18,26},{... | collective-permute-start | bytes 24584 | tf_op jit(solution)/shard_map/ppermute | solution.py:16
  341.1 10.0 collective-permute-start.24
  396.8 10.2 %collective-permute-start.28 = (f32[16,128]{0,1:T(8,128)S(1)}, f32[16,128]{0,1:T(8,128)S(1)}, u32[]{:S(2)}, u32[]{:S(2)}) collective-permute-start(f32[16,128]{0,1:T(8,128)S(1)} %get-tuple-element.69), channel_id=1, source_target_pairs={{0,8},{8,16},{16,24},{1,9},{9,17},{17,25},{2,10},{10,18},{18,26},{... | collective-permute-start | bytes 24584 | tf_op jit(solution)/shard_map/ppermute | solution.py:16
  452.7 10.0 collective-permute-start.32
  554.3 13.5 %collective-permute-start.39 = (f32[16,128]{1,0:T(8,128)S(1)}, f32[16,128]{1,0:T(8,128)S(1)}, u32[]{:S(2)}, u32[]{:S(2)}) collective-permute-start(f32[16,128]{1,0:T(8,128)S(1)} %bitcast.350), channel_id=1, source_target_pairs={{2,0},{4,2},{6,4},{3,1},{5,3},{7,5},{10,8},{12,10},{14,12},{11,9},... | collective-permute-start | bytes 24584 | tf_op jit(solution)/shard_map/ppermute | solution.py:16
  555.7 12.1 %collective-permute-start.38 = (f32[16,128]{1,0:T(8,128)S(1)}, f32[16,128]{1,0:T(8,128)S(1)}, u32[]{:S(2)}, u32[]{:S(2)}) collective-permute-start(f32[16,128]{1,0:T(8,128)S(1)} %bitcast.357), channel_id=1, source_target_pairs={{0,2},{2,4},{4,6},{1,3},{3,5},{5,7},{8,10},{10,12},{12,14},{9,11},... | collective-permute-start | bytes 24584 | tf_op jit(solution)/shard_map/ppermute | solution.py:16
  560.3 7.5 collective-permute-start.37
  561.7 7.4 collective-permute-start.36
  618.7 12.8 %collective-permute-start.43 = (f32[16,128]{1,0:T(8,128)S(1)}, f32[16,128]{1,0:T(8,128)S(1)}, u32[]{:S(2)}, u32[]{:S(2)}) collective-permute-start(f32[16,128]{1,0:T(8,128)S(1)} %bitcast.351), channel_id=1, source_target_pairs={{2,0},{4,2},{6,4},{3,1},{5,3},{7,5},{10,8},{12,10},{14,12},{11,9},... | collective-permute-start | bytes 24584 | tf_op jit(solution)/shard_map/ppermute | solution.py:16
  620.0 11.5 %collective-permute-start.42 = (f32[16,128]{1,0:T(8,128)S(1)}, f32[16,128]{1,0:T(8,128)S(1)}, u32[]{:S(2)}, u32[]{:S(2)}) collective-permute-start(f32[16,128]{1,0:T(8,128)S(1)} %bitcast.358), channel_id=1, source_target_pairs={{0,2},{2,4},{4,6},{1,3},{3,5},{5,7},{8,10},{10,12},{12,14},{9,11},... | collective-permute-start | bytes 24584 | tf_op jit(solution)/shard_map/ppermute | solution.py:16
  682.6 13.1 %collective-permute-start.47 = (f32[16,128]{1,0:T(8,128)S(1)}, f32[16,128]{1,0:T(8,128)S(1)}, u32[]{:S(2)}, u32[]{:S(2)}) collective-permute-start(f32[16,128]{1,0:T(8,128)S(1)} %bitcast.352), channel_id=1, source_target_pairs={{2,0},{4,2},{6,4},{3,1},{5,3},{7,5},{10,8},{12,10},{14,12},{11,9},... | collective-permute-start | bytes 24584 | tf_op jit(solution)/shard_map/ppermute | solution.py:16
  684.0 11.8 %collective-permute-start.46 = (f32[16,128]{1,0:T(8,128)S(1)}, f32[16,128]{1,0:T(8,128)S(1)}, u32[]{:S(2)}, u32[]{:S(2)}) collective-permute-start(f32[16,128]{1,0:T(8,128)S(1)} %bitcast.359), channel_id=1, source_target_pairs={{0,2},{2,4},{4,6},{1,3},{3,5},{5,7},{8,10},{10,12},{12,14},{9,11},... | collective-permute-start | bytes 24584 | tf_op jit(solution)/shard_map/ppermute | solution.py:16
  688.6 7.2 collective-permute-start.45
  746.6 13.1 %collective-permute-start.51 = (f32[16,128]{1,0:T(8,128)S(1)}, f32[16,128]{1,0:T(8,128)S(1)}, u32[]{:S(2)}, u32[]{:S(2)}) collective-permute-start(f32[16,128]{1,0:T(8,128)S(1)} %bitcast.353), channel_id=1, source_target_pairs={{2,0},{4,2},{6,4},{3,1},{5,3},{7,5},{10,8},{12,10},{14,12},{11,9},... | collective-permute-start | bytes 24584 | tf_op jit(solution)/shard_map/ppermute | solution.py:16
  748.0 11.8 %collective-permute-start.50 = (f32[16,128]{1,0:T(8,128)S(1)}, f32[16,128]{1,0:T(8,128)S(1)}, u32[]{:S(2)}, u32[]{:S(2)}) collective-permute-start(f32[16,128]{1,0:T(8,128)S(1)} %bitcast.360), channel_id=1, source_target_pairs={{0,2},{2,4},{4,6},{1,3},{3,5},{5,7},{8,10},{10,12},{12,14},{9,11},... | collective-permute-start | bytes 24584 | tf_op jit(solution)/shard_map/ppermute | solution.py:16
  752.6 7.2 collective-permute-start.49
  810.8 13.1 %collective-permute-start.55 = (f32[16,128]{1,0:T(8,128)S(1)}, f32[16,128]{1,0:T(8,128)S(1)}, u32[]{:S(2)}, u32[]{:S(2)}) collective-permute-start(f32[16,128]{1,0:T(8,128)S(1)} %bitcast.354), channel_id=1, source_target_pairs={{2,0},{4,2},{6,4},{3,1},{5,3},{7,5},{10,8},{12,10},{14,12},{11,9},... | collective-permute-start | bytes 24584 | tf_op jit(solution)/shard_map/ppermute | solution.py:16
  812.2 11.8 %collective-permute-start.54 = (f32[16,128]{1,0:T(8,128)S(1)}, f32[16,128]{1,0:T(8,128)S(1)}, u32[]{:S(2)}, u32[]{:S(2)}) collective-permute-start(f32[16,128]{1,0:T(8,128)S(1)} %bitcast.361), channel_id=1, source_target_pairs={{0,2},{2,4},{4,6},{1,3},{3,5},{5,7},{8,10},{10,12},{12,14},{9,11},... | collective-permute-start | bytes 24584 | tf_op jit(solution)/shard_map/ppermute | solution.py:16
  816.8 7.2 collective-permute-start.53
  874.8 13.1 %collective-permute-start.59 = (f32[16,128]{1,0:T(8,128)S(1)}, f32[16,128]{1,0:T(8,128)S(1)}, u32[]{:S(2)}, u32[]{:S(2)}) collective-permute-start(f32[16,128]{1,0:T(8,128)S(1)} %bitcast.355), channel_id=1, source_target_pairs={{2,0},{4,2},{6,4},{3,1},{5,3},{7,5},{10,8},{12,10},{14,12},{11,9},... | collective-permute-start | bytes 24584 | tf_op jit(solution)/shard_map/ppermute | solution.py:16
  876.2 11.8 %collective-permute-start.58 = (f32[16,128]{1,0:T(8,128)S(1)}, f32[16,128]{1,0:T(8,128)S(1)}, u32[]{:S(2)}, u32[]{:S(2)}) collective-permute-start(f32[16,128]{1,0:T(8,128)S(1)} %bitcast.362), channel_id=1, source_target_pairs={{0,2},{2,4},{4,6},{1,3},{3,5},{5,7},{8,10},{10,12},{12,14},{9,11},... | collective-permute-start | bytes 24584 | tf_op jit(solution)/shard_map/ppermute | solution.py:16
  939.1 13.4 %collective-permute-start.63 = (f32[16,128]{1,0:T(8,128)S(1)}, f32[16,128]{1,0:T(8,128)S(1)}, u32[]{:S(2)}, u32[]{:S(2)}) collective-permute-start(f32[16,128]{1,0:T(8,128)S(1)} %bitcast.356), channel_id=1, source_target_pairs={{2,0},{4,2},{6,4},{3,1},{5,3},{7,5},{10,8},{12,10},{14,12},{11,9},... | collective-permute-start | bytes 24584 | tf_op jit(solution)/shard_map/ppermute | solution.py:16
  940.5 12.0 %collective-permute-start.62 = (f32[16,128]{1,0:T(8,128)S(1)}, f32[16,128]{1,0:T(8,128)S(1)}, u32[]{:S(2)}, u32[]{:S(2)}) collective-permute-start(f32[16,128]{1,0:T(8,128)S(1)} %bitcast.363), channel_id=1, source_target_pairs={{0,2},{2,4},{4,6},{1,3},{3,5},{5,7},{8,10},{10,12},{12,14},{9,11},... | collective-permute-start | bytes 24584 | tf_op jit(solution)/shard_map/ppermute | solution.py:16
  945.2 7.3 collective-permute-start.61
  946.6 7.2 collective-permute-start.60
  (38 other events, 282.9 us)
where the time goes:
time: 1020 us; the launch traced here: 1010 us
  other arithmetic  464 us (45%)
  local copies, waits for them, and re-layouts  262 us (26%)
  starting transfers between devices  184 us (18%)
  waiting for transfers between devices  48.7 us (5%)
  blocking collectives  45.1 us (4%)
    scatter-add x7, other arithmetic, local(): arrived = jnp.zeros((dest_count, slot_total), jnp.float32).at[:, flat_tur...  285 us
    gather x9, local copies, waits for them, and re-layouts, select_cells(): picked = jnp.take(cells, flat_index, axis=1)  249 us
    ppermute x64, starting transfers between devices, passed_along(): return lax.ppermute(array, axis, pairs)  184 us
    select_n x9, other arithmetic, select_cells(): picked = jnp.take(cells, flat_index, axis=1)  56 us
    ppermute x64, waiting for transfers between devices, passed_along(): return lax.ppermute(array, axis, pairs)  48.7 us
    psum x1, blocking collectives, local(): gradient = lax.psum(block_term, ('gx', 'gy', 'dst'))  41.7 us
    reduce_sum x8, other arithmetic, local(): turn_counts = turn_counts + jnp.sum(turn_flow, axis=0)  40.7 us
    reduce_max x9, other arithmetic, local(): row_max = jnp.max(scores, axis=1)  25.1 us
  transfers between devices with their start and end apart: 64, of which 25 were waited for; matrix products, arithmetic and copies ran while one was open for 1% of the time, Pallas kernels for 0%

commit v1 on v0

--- a/solution.py
+++ b/solution.py
@@ -1,13 +1,757 @@
+import functools
+
 import jax
 import jax.numpy as jnp
 from jax import lax
+from jax.experimental import pallas as pl
+from jax.experimental.pallas import tpu as pltpu
 from jax.sharding import PartitionSpec as P
 
 HORIZON = 8
-
-
 NEG = -1e30
 START_COST = 100.0
+LANES = 128
+ROWS = 60
+RANKS = -(-ROWS // 16) * 16
+STEP = 19
+DEPTH = -(-ROWS // STEP) * STEP
+BLOCK_AXES = ("gx", "gy")
+
+LANE_PICK = lax.GatherDimensionNumbers(
+    offset_dims=(),
+    collapsed_slice_dims=(1,),
+    start_index_map=(1,),
+    operand_batching_dims=(0,),
+    start_indices_batching_dims=(0,),
+)
+
+
+def lane_gather(table, index):
+    return lax.gather(
+        table,
+        index[..., None],
+        LANE_PICK,
+        (1, 1),
+        mode=lax.GatherScatterMode.PROMISE_IN_BOUNDS,
+    )
+
+
+def tree_select(picked, bits):
+    level = list(picked)
+    for bit in bits:
+        if len(level) == 1:
+            break
+        nxt = []
+        for n in range(0, len(level), 2):
+            if n + 1 < len(level):
+                nxt.append(jnp.where(bit, level[n + 1], level[n]))
+            else:
+                nxt.append(level[n])
+        level = nxt
+    return level[0]
+
+
+def row_bits(index, count):
+    return [(index & (LANES << i)) != 0 for i in range(count)]
+
+
+def table_gather(table_rows, index):
+    lane = index & (LANES - 1)
+    bits = row_bits(index, max(len(table_rows) - 1, 1).bit_length())
+    return tree_select([lane_gather(row, lane) for row in table_rows], bits)
+
+
+def run_copies(copies):
+    for copy in copies:
+        copy.start()
+    for copy in copies:
+        copy.wait()
+
+
+def of_blocks(ref, half, row, per_block):
+    return ref[pl.ds(half * 8 * per_block + row, 8, stride=per_block), :]
+
+
+def whole_copies(pairs, sem):
+    return [pltpu.make_async_copy(src, dst, sem.at[n]) for n, (src, dst) in enumerate(pairs)]
+
+
+def by_core(what, mine, other):
+    first = lax.axis_index("dst") == 0
+    pl.when(first)(lambda: what(mine, other))
+    pl.when(jnp.logical_not(first))(lambda: what(other, mine))
+
+
+def own_block(grid_y):
+    return lax.axis_index("gx") * grid_y + lax.axis_index("gy")
+
+
+def target_mask(dest, half, chunk, per_block):
+    sub = lax.broadcasted_iota(jnp.int32, (8, LANES), 0)
+    lane = lax.broadcasted_iota(jnp.int32, (8, LANES), 1)
+    return (half * 8 + sub) * per_block + chunk * LANES + lane == dest
+
+
+def arrange_kernel(
+    succ_any, valid_any, border_any, reward_ref, out_any,
+    succ_ref, valid_ref, border_ref, out_ref, count_ref, first_ref, order_ref, inverse_ref, placed_ref,
+    pair_ref, lane_ref, code_ref, column_ref, acc_ref, sem
+):
+    run_copies(
+        whole_copies([(succ_any, succ_ref), (valid_any, valid_ref), (border_any, border_ref)], sem)
+    )
+    turns, width = succ_ref.shape
+    chunks = width // LANES
+    slots = chunks + 4
+    step = 2 * LANES
+    tops = 16
+    square = (LANES, LANES)
+    down = lax.broadcasted_iota(jnp.int32, square, 0)
+    along = lax.broadcasted_iota(jnp.int32, square, 1)
+    down_f, along_f = down.astype(jnp.float32), along.astype(jnp.float32)
+    before = down < along
+    unit = jnp.where(down == along, 1.0, 0.0)
+    lane_row = lax.broadcasted_iota(jnp.int32, (LANES, step), 0)
+    top_row = lax.broadcasted_iota(jnp.int32, (tops, step), 0)
+    rank_row = lax.broadcasted_iota(jnp.int32, (RANKS, step), 0).astype(jnp.float32)
+    last_dims = (((1,), (1,)), ((), ()))
+
+    def product(left, right):
+        return lax.dot_general(left, right, last_dims, preferred_element_type=jnp.float32)
+
+    def columns(rows):
+        return lax.dot_general(
+            unit, rows, last_dims, precision=lax.Precision.HIGHEST, preferred_element_type=jnp.float32
+        )
+
+    def summed_down(array):
+        return jnp.sum(array, axis=0, keepdims=True)
+
+    def place_of(row, col):
+        return summed_down(jnp.where((col > row) | ((col == row) & before), 1.0, 0.0))
+
+    def count(a, total):
+        for c in range(width // step):
+            cols = slice(c * step, (c + 1) * step)
+            u = succ_ref[pl.ds(a, 1), cols]
+            low = jnp.where(valid_ref[pl.ds(a, 1), cols] == 1, u & (LANES - 1), -1)
+            hot_low = jnp.where(low == lane_row, 1.0, 0.0).astype(jnp.bfloat16)
+            hot_top = jnp.where((u >> 7) == top_row, 1.0, 0.0).astype(jnp.bfloat16)
+            total = total + product(hot_top, hot_low)
+        return total
+
+    counts = lax.fori_loop(0, turns, count, jnp.zeros((tops, LANES), jnp.float32), unroll=2)
+    count_columns = columns(counts)
+    out_ref[...] = jnp.zeros_like(out_ref)
+    for ref in (count_ref, first_ref, order_ref, inverse_ref, placed_ref, pair_ref):
+        ref[...] = jnp.zeros_like(ref)
+    for n in range(slots):
+        i = n if n < chunks else n - chunks
+        place = place_of(counts[n : n + 1, :], count_columns[:, n : n + 1])
+        place = place if i % 2 == 0 else (LANES - 1.0) - place
+        if (i // 2) % 2:
+            place = jnp.where(place >= LANES // 2, place - LANES // 2, place + LANES // 2)
+        first_ref[n : n + 1, :] = place
+    first_columns = columns(first_ref[...])
+    for n in range(slots):
+        hit = first_columns[:, n : n + 1] == along_f
+        inverse_ref[n : n + 1, :] = summed_down(jnp.where(hit, down_f, 0.0))
+        placed_ref[n : n + 1, :] = summed_down(jnp.where(hit, count_columns[:, n : n + 1], 0.0))
+    local = summed_down(placed_ref[0:chunks, :])
+    room = -summed_down(placed_ref[chunks:tops, :])
+    pair_ref[0:1, :] = local
+    pair_ref[1:2, :] = room
+    pair = columns(pair_ref[...])
+    local_place, room_place = place_of(local, pair[:, 0:1]), place_of(room, pair[:, 1:2])
+    pair_ref[0:1, :] = local_place
+    pair_ref[1:2, :] = room_place
+    pair = columns(pair_ref[...])
+    goes = summed_down(jnp.where(pair[:, 1:2] == local_place, down_f, 0.0))
+    comes = summed_down(jnp.where(pair[:, 0:1] == room_place, down_f, 0.0))
+    full = (chunks, LANES)
+    comes = jnp.broadcast_to(comes, full).astype(jnp.int32)
+    goes = jnp.broadcast_to(goes, full)
+    order_ref[0:chunks, :] = lane_gather(goes, first_ref[0:chunks, :].astype(jnp.int32))
+    order_ref[chunks:tops, :] = first_ref[chunks:tops, :]
+    inverse_ref[0:chunks, :] = lane_gather(inverse_ref[0:chunks, :], comes)
+    placed_ref[0:chunks, :] = lane_gather(placed_ref[0:chunks, :], comes)
+    running = jnp.zeros((1, LANES), jnp.float32)
+    for n in range(slots):
+        count_ref[n : n + 1, :] = running
+        running = running + placed_ref[n : n + 1, :]
+        out_ref[ROWS + n : ROWS + n + 1, :] = running
+        out_ref[ROWS + slots + n : ROWS + slots + n + 1, :] = order_ref[n : n + 1, :]
+        out_ref[ROWS + 2 * slots + n : ROWS + 2 * slots + n + 1, :] = inverse_ref[n : n + 1, :]
+    for k in range(chunks):
+        cols = slice(k * LANES, (k + 1) * LANES)
+        u = succ_ref[:, cols]
+        rows = [jnp.broadcast_to(order_ref[n : n + 1, :], (turns, LANES)) for n in range(slots)]
+        lane = jnp.where(valid_ref[:, cols] == 1, table_gather(rows, u), -1.0)
+        code = jnp.where(lane >= 0.0, lane + ((u >> 7) * LANES).astype(jnp.float32), -1.0)
+        lane_ref[:, cols] = lane
+        code_ref[:, cols] = code
+        column_ref[cols, :] = columns(code)
+    acc_ref[...] = jnp.zeros_like(acc_ref)
+    earlier = jnp.where(
+        lax.broadcasted_iota(jnp.int32, (step, step), 0) < lax.broadcasted_iota(jnp.int32, (step, step), 1),
+        1.0,
+        0.0,
+    )
+    lane_row_f = lane_row.astype(jnp.float32)
+
+    def one_chunk(c, base):
+        start = pl.multiple_of(c * step, step)
+        cols = pl.ds(start, step)
+        s = start + lax.broadcasted_iota(jnp.int32, (1, step), 1)
+        source = [
+            (s & ~7).astype(jnp.float32).astype(jnp.bfloat16),
+            (s & 7).astype(jnp.float32).astype(jnp.bfloat16),
+        ]
+        for a in range(turns):
+            row = slice(a, a + 1)
+            hot = jnp.where(lane_ref[row, cols] == lane_row_f, 1.0, 0.0).astype(jnp.bfloat16)
+            hot_top = jnp.where((succ_ref[row, cols] >> 7) == top_row, 1.0, 0.0)
+            same = column_ref[cols, row] == code_ref[row, cols]
+            within = summed_down(jnp.where(same, earlier, 0.0))
+            coarse = (base.astype(jnp.int32) & ~127).astype(jnp.float32)
+            both = jnp.concatenate([coarse, base - coarse], axis=0).astype(jnp.bfloat16)
+            starts = jnp.dot(both, hot, preferred_element_type=jnp.float32)
+            begin = summed_down((starts[:tops] + starts[tops:]) * hot_top)
+            base = base + product(hot_top.astype(jnp.bfloat16), hot)
+            match = jnp.where(begin + within == rank_row, 1.0, 0.0).astype(jnp.bfloat16)
+            r = reward_ref[row, cols]
+            r1 = r.astype(jnp.bfloat16)
+            rest = r - r1.astype(jnp.float32)
+            r2 = rest.astype(jnp.bfloat16)
+            r3 = (rest - r2.astype(jnp.float32)).astype(jnp.bfloat16)
+            left = jnp.concatenate([match * piece for piece in (*source, r1, r2, r3)], axis=0)
+            acc_ref[...] += product(left, hot)
+        return base
+
+    lax.fori_loop(0, width // step, one_chunk, count_ref[...])
+    part = [acc_ref[i * RANKS : i * RANKS + ROWS, :] for i in range(5)]
+    share = out_ref.shape[0] // 2
+    out_ref[0:ROWS, :] = part[0] + part[1]
+    out_ref[share : share + ROWS, :] = (part[2] + part[3]) + part[4]
+    listed = columns(border_ref[...].astype(jnp.float32)).astype(jnp.int32)
+    for side in range(4):
+        for q in range(chunks):
+            found = jnp.where(listed[:, side : side + 1] == along + q * LANES, down_f + 1.0, 0.0)
+            row = share + ROWS + side * chunks + q
+            out_ref[row : row + 1, :] = summed_down(found)
+    half = out_ref.at[pl.ds(pl.multiple_of(lax.axis_index("dst") * share, 8), share)]
+    blocks = out_any.shape[0] // share
+    run_copies(whole_copies([(half, out_any.at[pl.ds(b * share, share)]) for b in range(blocks)], sem))
+
+
+def graph_kernel(
+    weight_ref, feature_any, succ_any, valid_any, border_any, anchor_any, out_ref, reward_ref,
+    feature_ref, succ_ref, valid_ref, border_ref, anchor_ref, part_ref, split_ref, sem
+):
+    run_copies(
+        whole_copies(
+            [
+                (feature_any, feature_ref),
+                (succ_any, succ_ref),
+                (valid_any, valid_ref),
+                (border_any, border_ref),
+                (anchor_any, anchor_ref),
+            ],
+            sem,
+        )
+    )
+    turns, width = succ_ref.shape
+    chunks = width // LANES
+    edges = turns * chunks
+    part_ref[edges : edges + 8, :] = jnp.zeros((8, LANES), jnp.float32)
+    part_ref[edges : edges + 4, :] = border_ref[...].astype(jnp.float32)
+    first_core = lax.axis_index("dst") == 0
+    for q in range(chunks):
+        cols = slice(q * LANES, (q + 1) * LANES)
+        cost = weight_ref[0] * feature_ref[0, :, cols].astype(jnp.float32)
+        for f in range(1, feature_ref.shape[0]):
+            cost = cost + weight_ref[f] * feature_ref[f, :, cols].astype(jnp.float32)
+        reward_ref[:, cols] = -cost
+        masked = jnp.where(valid_ref[:, cols] == 1, -cost, NEG)
+        turn_to = succ_ref[:, cols].astype(jnp.float32)
+        part_ref[pl.ds(q, turns, chunks), :] = jnp.where(first_core, masked, turn_to)
+        split_ref[pl.ds(q, anchor_ref.shape[0], chunks), :] = anchor_ref[:, cols]
+    blocks = anchor_ref.shape[0]
+    size, common = out_ref.shape[0] // blocks, part_ref.shape[0]
+    for b in range(blocks):
+        out_ref[b * size : b * size + common, :] = part_ref[...]
+        out_ref[b * size + common : (b + 1) * size, :] = split_ref[b * chunks : (b + 1) * chunks, :]
+
+
+def value_kernel(
+    grid_y, dest_ref, mine_ref, other_ref, ext_ref, raised_ref, max_ref, inv_ref,
+    reward, index, border, side_pad, spare_ref
+):
+    halves = ext_ref.shape[0]
+    size = mine_ref.shape[0] // (8 * halves)
+    chunks = ext_ref.shape[1] - 4
+    turns = raised_ref.shape[1] // chunks
+    edges = turns * chunks
+    per_block = chunks * LANES
+    dest = dest_ref[own_block(grid_y)]
+    side_pad[...] = jnp.zeros_like(side_pad)
+    sub = lax.broadcasted_iota(jnp.int32, (8, LANES), 0)
+    lane = lax.broadcasted_iota(jnp.int32, (8, LANES), 1)
+    dest_block, dest_place = lax.div(dest, per_block), lax.rem(dest, per_block)
+
+    def unpack(first, second):
+        for h in range(halves):
+
+            def rows(i, carry, h=h):
+                reward[h, i] = of_blocks(first, h, i, size)
+                index[h, i] = of_blocks(second, h, i, size).astype(jnp.int32)
+                return carry
+
+            lax.fori_loop(0, edges, rows, 0, unroll=8)
+            for side in range(4):
+                border[h, side] = of_blocks(first, h, edges + side, size).astype(jnp.int32)
+
+    by_core(unpack, mine_ref, other_ref)
+    for h in range(halves):
+        for side in range(4):
+            found = (border[h, side] == dest_place) & (h * 8 + sub == dest_block)
+            entry = jnp.max(jnp.where(found, lane + 1, 0).astype(jnp.float32), axis=1, keepdims=True)
+            side_pad[side, 8 + 8 * h : 16 + 8 * h, :] = jnp.broadcast_to(entry, (8, LANES))
+    shifts = ((1, -grid_y), (0, grid_y), (3, -1), (2, 1))
+
+    def shown(h, side):
+        facing, by = shifts[side]
+        start = 8 + 8 * h + by
+        return side_pad[facing, start : start + 8, :]
+
+    def dest_index(h):
+        where = jnp.where(h * 8 + sub == dest_block, dest_place, -1)
+        for side in range(4):
+            entry = shown(h, side).astype(jnp.int32)
+            where = jnp.where(entry > 0, per_block + side * LANES + entry - 1, where)
+        return where
+
+    def bring_halo(values):
+        for h in range(halves):
+            table = [values[h, q] for q in range(chunks)]
+            for side in range(4):
+                side_pad[side, 8 + 8 * h : 16 + 8 * h, :] = table_gather(table, border[h, side])
+        for h in range(halves):
+            for side in range(4):
+                values[h, chunks + side] = shown(h, side)
+
+    def summed(out):
+        top = functools.reduce(jnp.maximum, out)
+        raised = [jnp.exp(score - top) for score in out]
+        return top, raised, functools.reduce(jnp.add, raised)
+
+    def scores_of(values, h, q):
+        tables = [values[h, r] for r in range(chunks + 4)]
+        out = []
+        for a in range(turns):
+            rows = tables if a else tables[:chunks]
+            out.append(reward[h, a * chunks + q] + table_gather(rows, index[h, a * chunks + q]))
+        return summed(out)
+
+    def store_value(h, q, top, total, into):
+        value = top + jnp.log(total)
+        into[h, q] = jnp.where(target_mask(dest, h, q, per_block), 0.0, value)
+
+    wanted = [dest_index(h) for h in range(halves)]
+
+    def first_chunk(q, inner):
+        for h in range(halves):
+            out = []
+            for a in range(turns):
+                before = jnp.where(index[h, a * chunks + q] == wanted[h], 0.0, -START_COST)
+                out.append(reward[h, a * chunks + q] + before)
+            top, _, total = summed(out)
+            store_value(h, q, top, total, spare_ref)
+        return inner
+
+    lax.fori_loop(0, chunks, first_chunk, 0, unroll=2)
+
+    def backup(values, into):
+        bring_halo(values)
+
+        def one_chunk(q, inner):
+            for h in range(halves):
+                top, _, total = scores_of(values, h, q)
+                store_value(h, q, top, total, into)
+            return inner
+
+        lax.fori_loop(0, chunks, one_chunk, 0, unroll=chunks)
+
+    def two_backups(step, carry):
+        backup(spare_ref, ext_ref)
+        backup(ext_ref, spare_ref)
+        return carry
+
+    lax.fori_loop(0, (HORIZON - 2) // 2, two_backups, 0)
+    backup(spare_ref, ext_ref)
+    bring_halo(ext_ref)
+
+    def last_chunk(q, inner):
+        for h in range(halves):
+            top, raised, total = scores_of(ext_ref, h, q)
+            max_ref[h, q] = top
+            inv_ref[h, q] = 1.0 / total
+            for a in range(turns):
+                raised_ref[h, a * chunks + q] = raised[a]
+        return inner
+
+    lax.fori_loop(0, chunks, last_chunk, 0, unroll=chunks)
+
+
+def push_kernel(
+    grid_y, scale, dest_ref, mine_ref, other_ref, graph_mine, graph_other, ext_ref, raised_ref, max_ref,
+    inv_ref, keep_ref, send_ref, ends, order, values, source, slot, policy, back, scaled, total, arrived, side_pad, raw
+):
+    halves = ext_ref.shape[0]
+    blocks = 8 * halves
+    size, share = graph_mine.shape[0] // blocks, mine_ref.shape[0] // blocks
+    chunks = max_ref.shape[1]
+    edges = raised_ref.shape[1]
+    turns = edges // chunks
+    per_block = chunks * LANES
+    slots = chunks + 4
+    dest = dest_ref[own_block(grid_y)]
+    core = lax.axis_index("dst")
+    side_pad[...] = jnp.zeros_like(side_pad)
+
+    def unpack(first, second):
+        for h in range(halves):
+            for n in range(slots):
+                ends[h, n] = of_blocks(first, h, ROWS + n, share)
+                order[h, n] = of_blocks(first, h, ROWS + slots + n, share).astype(jnp.int32)
+                inverse = of_blocks(first, h, ROWS + 2 * slots + n, share).astype(jnp.int32)
+                values[h, n] = lane_gather(ext_ref[h, n], inverse)
+
+            def rows(r, carry, h=h):
+                source[h, r] = of_blocks(first, h, r, share).astype(jnp.int32)
+                policy[h, r] = of_blocks(second, h, r, share)
+                return carry
+
+            lax.fori_loop(0, ROWS, rows, 0, unroll=6)
+            for r in range(ROWS, DEPTH):
+                source[h, r] = jnp.zeros((8, LANES), jnp.int32)
+                policy[h, r] = jnp.zeros((8, LANES), jnp.float32)
+            for n in range(4 * chunks):
+                back[h, n] = of_blocks(second, h, ROWS + n, share).astype(jnp.int32) - 1
+
+    by_core(unpack, mine_ref, other_ref)
+    deepest = jnp.max(functools.reduce(jnp.maximum, [ends[h, slots - 1] for h in range(halves)]))
+    deepest = deepest.astype(jnp.int32)
+    fits = deepest <= ROWS
+    steps = lax.div(jnp.minimum(deepest, ROWS) + (STEP - 1), STEP)
+    shifts = ((1, -grid_y), (0, grid_y), (3, -1), (2, 1))
+
+    def shown(h, side):
+        facing, by = shifts[side]
+        start = 8 + 8 * h + by
+        return side_pad[facing, start : start + 8, :]
+
+    @pl.when(jnp.logical_not(fits))
+    def _():
+        for h in range(halves):
+            for n in range(slots):
+                order[h, n] = lax.broadcasted_iota(jnp.int32, (8, LANES), 1)
+
+    for h in range(halves):
+        for side in range(4):
+            side_pad[side, 8 + 8 * h : 16 + 8 * h, :] = order[h, chunks + side].astype(jnp.float32)
+    for h in range(halves):
+        for side in range(4):
+            lanes = shown(h, side).astype(jnp.int32)
+            for q in range(chunks):
+                entry = back[h, side * chunks + q]
+                back[h, side * chunks + q] = jnp.where(
+                    entry >= 0, lane_gather(lanes, jnp.maximum(entry, 0)), -1
+                )
+
+    def prepare(t, carry):
+        for i in range(STEP):
+            for h in range(halves):
+                r = t * STEP + i
+                src = source[h, r]
+                place = r.astype(jnp.float32)
+                row = functools.reduce(
+                    jnp.add, [jnp.where(ends[h, n] <= place, 1, 0) for n in range(slots)]
+                )
+                slot[h, r] = row
+                bits = [(row & (1 << n)) != 0 for n in range(4)]
+                picked = tree_select([values[h, n] for n in range(slots)], bits)
+                top = table_gather([max_ref[h, q] for q in range(chunks)], src)
+                policy[h, r] = jnp.exp(policy[h, r] + picked - top)
+        return carry
+
+    lax.fori_loop(0, steps, prepare, 0)
+    for h in range(halves):
+        for q in range(chunks):
+            own = of_blocks(graph_mine, h, size - chunks + q, size)
+            first = jnp.where(target_mask(dest, h, q, per_block), 0.0, own)
+            total[h, q] = first
+            scaled[h, q] = first * inv_ref[h, q]
+
+    @pl.when(jnp.logical_not(fits))
+    def _():
+        def keep_turns(first, second):
+            for h in range(halves):
+
+                def rows(e, carry, h=h):
+                    raw[h, e] = of_blocks(second, h, e, size).astype(jnp.int32)
+                    return carry
+
+                lax.fori_loop(0, edges, rows, 0)
+
+        by_core(keep_turns, graph_mine, graph_other)
+
+    zero = jnp.zeros((8, LANES), jnp.float32)
+
+    def keep(h):
+        for side in range(4):
+            side_pad[side, 8 + 8 * h : 16 + 8 * h, :] = arrived[h, chunks + side]
+
+    def add_flow(acc, row, flow):
+        return [acc[n] + jnp.where(row == n, flow, 0.0) for n in range(slots)]
+
+    def sum_arranged():
+        for h in range(halves):
+            for n in range(slots):
+                arrived[h, n] = zero
+
+        def one_step(t, carry):
+            for h in range(halves):
+                table = [scaled[h, q] for q in range(chunks)]
+                acc = [arrived[h, n] for n in range(slots)]
+                for i in range(STEP):
+                    r = t * STEP + i
+                    flow = table_gather(table, source[h, r]) * policy[h, r]
+                    acc = add_flow(acc, slot[h, r], flow)
+                for n in range(slots):
+                    arrived[h, n] = acc[n]
+            return carry
+
+        lax.fori_loop(0, steps, one_step, 0)
+        for h in range(halves):
+            keep(h)
+
+    def sum_turned():
+        lane = lax.broadcasted_iota(jnp.int32, (8, LANES), 1)
+        for h in range(halves):
+
+            def one_edge_row(e, acc, h=h):
+                flow = scaled[h, lax.rem(e, chunks)] * raised_ref[h, e]
+                where = raw[h, e]
+
+                def one_turn(k, state):
+                    flow, where, acc = state[0], state[1], list(state[2:])
+                    here = jnp.where((where & (LANES - 1)) == lane, where >> 7, -1)
+                    acc = add_flow(acc, here, flow)
+                    return (pltpu.roll(flow, 1, 1), pltpu.roll(where, 1, 1), *acc)
+
+                return tuple(lax.fori_loop(0, LANES, one_turn, (flow, where, *acc))[2:])
+
+            for n, value in enumerate(lax.fori_loop(0, edges, one_edge_row, (zero,) * slots)):
+                arrived[h, n] = value
+            keep(h)
+
+    def push(round_index, carry):
+        pl.when(fits)(sum_arranged)
+        pl.when(jnp.logical_not(fits))(sum_turned)
+        for h in range(halves):
+            landed = [shown(h, side) for side in range(4)]
+            for q in range(chunks):
+                value = lane_gather(arrived[h, q], order[h, q])
+                for side in range(4):
+                    entry = back[h, side * chunks + q]
+                    got = lane_gather(landed[side], jnp.maximum(entry, 0))
+                    value = value + jnp.where(entry >= 0, got, 0.0)
+                value = jnp.where(target_mask(dest, h, q, per_block), 0.0, value)
+                total[h, q] = total[h, q] + value
+                scaled[h, q] = value * inv_ref[h, q]
+        return carry
+
+    lax.fori_loop(0, HORIZON - 1, push, 0)
+    for h in range(halves):
+        for q in range(chunks):
+            weight = total[h, q] * inv_ref[h, q] * scale
+            for part, out_ref in ((core, keep_ref), (1 - core, send_ref)):
+                for a in range(turns // 2):
+                    value = weight * raised_ref[h, (part * (turns // 2) + a) * chunks + q]
+                    start = h * 4 * edges + a * chunks + q
+                    out_ref[pl.ds(start, 8, stride=edges // 2), :] = value
+
+
+VMEM_SPEC = pl.BlockSpec(memory_space=pltpu.VMEM)
+SMEM_SPEC = pl.BlockSpec(memory_space=pltpu.SMEM)
+HBM_SPEC = pl.BlockSpec(memory_space=pltpu.HBM)
+PARAMS = pltpu.CompilerParams(vmem_limit_bytes=48 * 1024 * 1024)
+
+
+def f32(*shape):
+    return jax.ShapeDtypeStruct(shape, jnp.float32)
+
+
+def call_graph(cost_weights, features, successors, turn_valid, border_lists, anchors):
+    turns, width = successors.shape
+    blocks = anchors.shape[0]
+    chunks = width // LANES
+    rows = turns * chunks + 8
+    return pl.pallas_call(
+        graph_kernel,
+        out_shape=(f32(blocks * (rows + chunks), LANES), f32(turns, width)),
+        in_specs=[SMEM_SPEC] + [HBM_SPEC] * 5,
+        out_specs=(VMEM_SPEC, VMEM_SPEC),
+        scratch_shapes=[
+            pltpu.VMEM(features.shape, features.dtype),
+            pltpu.VMEM(successors.shape, jnp.int32),
+            pltpu.VMEM(turn_valid.shape, jnp.int32),
+            pltpu.VMEM(border_lists.shape, jnp.int32),
+            pltpu.VMEM(anchors.shape, jnp.float32),
+            pltpu.VMEM((rows, LANES), jnp.float32),
+            pltpu.VMEM((blocks * chunks, LANES), jnp.float32),
+            pltpu.SemaphoreType.DMA((5,)),
+        ],
+        compiler_params=pltpu.CompilerParams(vmem_limit_bytes=63 * 1024 * 1024),
+        name="own_graph",
+    )(cost_weights, features, successors, turn_valid, border_lists, anchors)
+
+
+def arranged_rows(chunks):
+    most = ROWS + max(3 * (chunks + 4), 4 * chunks)
+    return -(-most // 8) * 8
+
+
+def call_arrange(successors, turn_valid, border_lists, reward, blocks):
+    chunks = successors.shape[1] // LANES
+    share = arranged_rows(chunks)
+    return pl.pallas_call(
+        arrange_kernel,
+        out_shape=f32(blocks * share, LANES),
+        in_specs=[HBM_SPEC] * 3 + [VMEM_SPEC],
+        out_specs=HBM_SPEC,
+        scratch_shapes=[
+            pltpu.VMEM(successors.shape, jnp.int32),
+            pltpu.VMEM(turn_valid.shape, jnp.int32),
+            pltpu.VMEM(border_lists.shape, jnp.int32),
+            pltpu.VMEM((2 * share, LANES), jnp.float32),
+            *[pltpu.VMEM((16, LANES), jnp.float32)] * 5,
+            pltpu.VMEM((8, LANES), jnp.float32),
+            pltpu.VMEM(successors.shape, jnp.float32),
+            pltpu.VMEM(successors.shape, jnp.float32),
+            pltpu.VMEM(successors.shape[::-1], jnp.float32),
+            pltpu.VMEM((5 * RANKS, LANES), jnp.float32),
+            pltpu.SemaphoreType.DMA((blocks,)),
+        ],
+        compiler_params=PARAMS,
+        cost_estimate=pl.CostEstimate(flops=4_000_000_000, bytes_accessed=400_000, transcendentals=0),
+        name="arrange_turns",
+    )(successors, turn_valid, border_lists, reward)
+
+
+def call_values(destinations, mine, other, blocks, grid_y, turns, chunks):
+    halves = blocks // 8
+    edges = turns * chunks
+    return pl.pallas_call(
+        functools.partial(value_kernel, grid_y),
+        out_shape=(
+            f32(halves, chunks + 4, 8, LANES),
+            f32(halves, edges, 8, LANES),
+            f32(halves, chunks, 8, LANES),
+            f32(halves, chunks, 8, LANES),
+        ),
+        in_specs=[SMEM_SPEC, VMEM_SPEC, VMEM_SPEC],
+        out_specs=(VMEM_SPEC,) * 4,
+        scratch_shapes=[
+            pltpu.VMEM((halves, edges, 8, LANES), jnp.float32),
+            pltpu.VMEM((halves, edges, 8, LANES), jnp.int32),
+            pltpu.VMEM((halves, 4, 8, LANES), jnp.int32),
+            pltpu.VMEM((4, blocks + 16, LANES), jnp.float32),
+            pltpu.VMEM((halves, chunks + 4, 8, LANES), jnp.float32),
+        ],
+        compiler_params=PARAMS,
+        cost_estimate=pl.CostEstimate(flops=40_000_000, bytes_accessed=40_000_000, transcendentals=2_000_000),
+        name="soft_values",
+    )(destinations, mine, other)
+
+
+def call_push(destinations, mine, other, graph_mine, graph_other, ext, raised, top, inv, grid_y, scale):
+    halves, edges = raised.shape[:2]
+    blocks = 8 * halves
+    chunks = top.shape[1]
+
+    def vmem(rows, dtype=jnp.float32):
+        return pltpu.VMEM((halves, rows, 8, LANES), dtype)
+
+    return pl.pallas_call(
+        functools.partial(push_kernel, grid_y, scale),
+        out_shape=(f32(blocks * edges // 2, LANES),) * 2,
+        in_specs=[SMEM_SPEC] + [VMEM_SPEC] * 8,
+        out_specs=(VMEM_SPEC,) * 2,
+        scratch_shapes=[
+            vmem(chunks + 4),
+            vmem(chunks + 4, jnp.int32),
+            vmem(chunks + 4),
+            vmem(DEPTH, jnp.int32),
+            vmem(DEPTH, jnp.int32),
+            vmem(DEPTH),
+            vmem(4 * chunks, jnp.int32),
+            vmem(chunks),
+            vmem(chunks),
+            vmem(chunks + 4),
+            pltpu.VMEM((4, blocks + 16, LANES), jnp.float32),
+            vmem(edges, jnp.int32),
+        ],
+        compiler_params=PARAMS,
+        name="push_mass",
+    )(destinations, mine, other, graph_mine, graph_other, ext, raised, top, inv)
+
+
+def to_blocks(array):
+    return lax.all_to_all(array, BLOCK_AXES, 0, 0, tiled=True)
+
+
+def other_core(array):
+    return lax.ppermute(array, "dst", [(0, 1), (1, 0)])
+
+
+def per_destination(
+    features, cost_weights, successors, turn_valid, border_lists, destinations, anchors, demo_counts
+):
+    turns, own_count = successors.shape
+    chunks = own_count // LANES
+    edges = turns * chunks
+    grid_y = lax.axis_size("gy")
+    blocks = lax.axis_size("gx") * grid_y
+    groups = lax.axis_size("dst")
+    pieces, reward = call_graph(cost_weights, features, successors, turn_valid, border_lists, anchors)
+    graph = to_blocks(pieces)
+    arranged = call_arrange(successors, turn_valid, border_lists, reward, blocks)
+    core = lax.axis_index("dst")
+    demo_term = jnp.where(turn_valid == 1, demo_counts, 0).astype(jnp.float32) / 3.0
+    own_feats = lax.dynamic_slice_in_dim(features, core * (turns // 2), turns // 2, axis=1)
+    graph = lax.optimization_barrier((graph, arranged))[0]
+    arranged = to_blocks(arranged)
+    graph = (graph, other_core(graph))
+    values = call_values(destinations, *graph, blocks, grid_y, turns, chunks)
+    arranged, own_feats, demo_term, *values = lax.optimization_barrier(
+        (arranged, own_feats, demo_term, *values)
+    )
+    arranged = (arranged, other_core(arranged))
+    scale = 1.0 / (anchors.shape[0] * groups * HORIZON)
+    kept, sent = call_push(destinations, *arranged, *graph, *values, grid_y, scale)
+    halved = (kept + other_core(sent)).reshape(blocks, edges // 2, LANES)
+    half = jnp.sum(to_blocks(halved), axis=0)
+    other = other_core(half)
+    part = (turns // 2, own_count)
+    own_gap = lax.dynamic_slice_in_dim(demo_term, core * part[0], part[0]) - half.reshape(part)
+    own_feats = own_feats.astype(jnp.float32)
+    block_term = jnp.sum(own_gap[None] * own_feats, axis=(1, 2)) / (own_count * blocks)
+    terms = jnp.broadcast_to(block_term, (groups * blocks, 1, block_term.shape[0]))
+    terms = lax.all_to_all(terms, (*BLOCK_AXES, "dst"), 0, 0, tiled=True)
+    visits = jnp.concatenate([jnp.where(core == 0, half, other), jnp.where(core == 0, other, half)])
+    return demo_term - visits.reshape(turns, own_count), jnp.sum(terms, axis=(0, 1))
 
 
 def passed_along(array, axis, by):
@@ -47,7 +791,7 @@
     return jnp.where(usable[None], scores, NEG)
 
 
-def local(
+def per_block(
     features, cost_weights, successors, turn_valid, border_lists, destinations, anchors, demo_counts
 ):
     own_count = successors.shape[1]
@@ -97,6 +841,23 @@
     return (count_gap, gradient)
 
 
+def local(features, cost_weights, successors, turn_valid, border_lists, destinations, anchors, demo_counts):
+    args = (
+        features, cost_weights, successors, turn_valid, border_lists, destinations, anchors, demo_counts
+    )
+    blocks = lax.axis_size("gx") * lax.axis_size("gy")
+    fits = (
+        anchors.shape[0] == blocks
+        and blocks % 8 == 0
+        and lax.axis_size("dst") == 2
+        and lax.axis_size("gx") in (2, 4, 8)
+        and lax.axis_size("gy") in (2, 4, 8)
+        and successors.shape[1] == 8 * LANES
+        and border_lists.shape[1] == LANES
+    )
+    return per_destination(*args) if fits else per_block(*args)
+
+
 def solution(mesh):
     in_specs = (
         P(None, None, ("gx", "gy")),

time: 1020 us -> 107 us (0.10); the launches traced: 1010 us -> 106 us
  other arithmetic: 464 us -> 1.57 us
  local copies, waits for them, and re-layouts: 262 us -> 1.42 us
  starting transfers between devices: 184 us -> 15.1 us
  Pallas kernels: 0 us -> 50.4 us
  waiting for transfers between devices: 48.7 us -> 20.1 us
  blocking collectives: 45.1 us -> 17 us
    scatter-add x14 -> x0, other arithmetic: 309 us -> none  [the longest x7 285 us: local(): arrived = jnp.zeros((dest_count, slot_total), jnp.float32).at[:, flat_tur...]
    gather x18 -> x0, local copies, waits for them, and re-layouts: 259 us -> none  [the longest x9 249 us: select_cells(): picked = jnp.take(cells, flat_index, axis=1)]
    ppermute x64 -> x4, starting transfers between devices: 184 us -> 0.35 us  [other_core(): return lax.ppermute(array, 'dst', [(0, 1), (1, 0)])]
    reduce_sum x19 -> x3, other arithmetic: 67.8 us -> 0.88 us  [the longest x1 0.53 us: per_destination(): jnp.sum(terms, axis=(0, 1))]
    select_n x18 -> x1, other arithmetic: 56.5 us -> 0.01 us  [per_destination(): jnp.where(core == 0, half, other)]
    pallas_call x0 -> x4, Pallas kernels: none -> 50.4 us  [the longest x1 18.5 us: call_values(): pl.pallas_call(functools.partial(value_kernel, grid_y), out_shape=(f32(ha...]
    psum x2 -> x0, blocking collectives: 45.1 us -> none  [the longest x1 41.7 us: local(): gradient = lax.psum(block_term, ('gx', 'gy', 'dst'))]
    ppermute x64 -> x4, waiting for transfers between devices: 48.7 us -> 4.98 us  [other_core(): return lax.ppermute(array, 'dst', [(0, 1), (1, 0)])]
  transfers between devices with their start and end apart: 64 -> 7, of which waited for: 25 -> 6; matrix products, arithmetic and copies ran while one was open for 1% -> 2% of each run, Pallas kernels for 0% -> 28%
where the time goes in v1:
time: 107 us; the launch traced here: 106 us
  Pallas kernels  50.4 us (47%)
  waiting for transfers between devices  20.1 us (19%)
  blocking collectives  17 us (16%)
  starting transfers between devices  15.1 us (14%)
  other arithmetic  1.57 us (1%)
  local copies, waits for them, and re-layouts  1.42 us (1%)
    pallas_call x1, Pallas kernels, call_values(): pl.pallas_call(functools.partial(value_kernel, grid_y), out_shape=(f32(ha...  18.5 us
    pallas_call x1, Pallas kernels, call_push(): pl.pallas_call(functools.partial(push_kernel, grid_y, scale), out_shape=(...  17.7 us
    all_to_all x1, blocking collectives, to_blocks(): return lax.all_to_all(array, BLOCK_AXES, 0, 0, tiled=True)  17 us
    all_to_all x2, starting transfers between devices, to_blocks(): return lax.all_to_all(array, BLOCK_AXES, 0, 0, tiled=True)  12.2 us
    pallas_call x1, Pallas kernels, call_arrange(): pl.pallas_call(arrange_kernel, out_shape=f32(blocks * share, LANES), in_s...  11.4 us
    all_to_all x2, waiting for transfers between devices, to_blocks(): return lax.all_to_all(array, BLOCK_AXES, 0, 0, tiled=True)  8.09 us
    all_to_all x1, waiting for transfers between devices, per_destination(): terms = lax.all_to_all(terms, (*BLOCK_AXES, 'dst'), 0, 0, tiled=True)  7.06 us
    ppermute x4, waiting for transfers between devices, other_core(): return lax.ppermute(array, 'dst', [(0, 1), (1, 0)])  4.98 us
  transfers between devices with their start and end apart: 7, of which 6 were waited for; matrix products, arithmetic and copies ran while one was open for 2% of the time, Pallas kernels for 28%

profile of v1, /device:TPU:0, one launch (start us, length us, event | category | flops | bytes accessed | tf_op | source)
XLA Modules:
  0.0 106.4 jit_solution(12273846165367259717)
XLA Ops:
  0.6 2.8 %own_graph.1 = (f32[1280,128]{1,0:T(8,128)}, f32[8,1024]{1,0:T(8,128)}) custom-call(f32[32]{0:T(128)} %weight_ref.1, bf16[32,8,1024]{2,1,0:T(8,128)(2,1)} %feature_any.1, s32[8,1024]{1,0:T(8,128)} %succ_any.3, s32[8,1024]{1,0:T(8,128)} %valid_any.3, s32[4,128]{1,0:T(4,128)} %border_any.3, f32[16,1024]{1,0:T(8,128)} %anchor_any.1), custom_call_target="tpu_custom_call" | custom-call | tf_op jit(solution)/shard_map/own_graph/pallas_call | solution.py:601
  3.4 0.0 copy-start
  3.4 0.0 copy-start.1
  3.5 0.0 copy-start.2
  3.5 0.0 copy-start.4
  3.5 8.5 %all-to-all-start.1 = ((f32[16,80,128]{2,1,0:T(8,128)}), f32[16,80,128]{2,1,0:T(8,128)S(1)}, u32[]{:S(2)}, u32[]{:S(2)}) async-start(f32[16,80,128]{2,1,0:T(8,128)} %bitcast.12), calls=%async_computation.1 | async-start | bytes 1310720 | tf_op jit(solution)/shard_map/all_to_all | solution.py:712
  11.9 0.0 copy-done
  12.0 0.0 copy-done.1
  12.0 11.4 %arrange_turns.1 = f32[1536,128]{1,0:T(8,128)} custom-call(s32[8,1024]{1,0:T(8,128)S(1)} %copy-done.1, s32[8,1024]{1,0:T(8,128)S(1)} %copy-done, s32[4,128]{1,0:T(4,128)S(1)} %copy-done.2, f32[8,1024]{1,0:T(8,128)S(1)} %copy-done.4), custom_call_target="tpu_custom_call" | custom-call | flops 4000000000 | bytes 400000 | tf_op jit(solution)/shard_map/arrange_turns/pallas_call | solution.py:629
  23.4 7.5 %all-to-all-done.1 = f32[16,80,128]{2,1,0:T(8,128)S(1)} async-done(((f32[16,80,128]{2,1,0:T(8,128)}), f32[16,80,128]{2,1,0:T(8,128)S(1)}, u32[]{:S(2)}, u32[]{:S(2)}) %all-to-all-start.1) | async-done | bytes 655392 | tf_op jit(solution)/shard_map/all_to_all | solution.py:712
  30.9 3.7 %all-to-all-start = ((f32[16,96,128]{2,1,0:T(8,128)}), f32[16,96,128]{2,1,0:T(8,128)S(1)}, u32[]{:S(2)}, u32[]{:S(2)}) async-start(f32[16,96,128]{2,1,0:T(8,128)} %bitcast), calls=%async_computation | async-start | bytes 1572864 | tf_op jit(solution)/shard_map/all_to_all | solution.py:712
  34.7 0.1 collective-permute-start
  34.8 0.0 copy-start.6
  34.8 0.1 constant_dynamic-slice_fusion
  35.0 0.6 copy-done.6
  35.6 1.3 %collective-permute-done.other_ref.graph_other = f32[1280,128]{1,0:T(8,128)S(1)} collective-permute-done((f32[1280,128]{1,0:T(8,128)S(1)}, f32[1280,128]{1,0:T(8,128)S(1)}, u32[]{:S(2)}, u32[]{:S(2)}) %collective-permute-start) | collective-permute-done | bytes 655392 | tf_op jit(solution)/shard_map/ppermute | solution.py:716
  36.9 18.5 %soft_values.1 = (f32[2,12,8,128]{3,2,1,0:T(8,128)S(1)}, f32[2,64,8,128]{3,2,1,0:T(8,128)S(1)}, f32[2,8,8,128]{3,2,1,0:T(8,128)S(1)}, f32[2,8,8,128]{3,2,1,0:T(8,128)S(1)}) custom-call(s32[16]{0:T(128)S(1)} %copy-done.3, f32[1280,128]{1,0:T(8,128)S(1)} %bitcast.9, f32[1280,128]{1,0:T(8,128)S(1)} %collective-permute-done.other_ref.graph_other), custom_call_target="tpu_custom_call" | custom-call | flops 40000000 | bytes 40000000 | tf_op jit(solution)/shard_map/soft_values/pallas_call | solution.py:656
  55.4 0.6 all-to-all-done
  55.9 0.0 collective-permute-start.1
  55.9 2.3 %collective-permute-done.1.other_ref = f32[1536,128]{1,0:T(8,128)S(1)} collective-permute-done((f32[1536,128]{1,0:T(8,128)S(1)}, f32[1536,128]{1,0:T(8,128)S(1)}, u32[]{:S(2)}, u32[]{:S(2)}) %collective-permute-start.1) | collective-permute-done | bytes 786464 | tf_op jit(solution)/shard_map/ppermute | solution.py:716
  58.2 17.7 %push_mass.1 = (f32[512,128]{1,0:T(8,128)S(1)}, f32[512,128]{1,0:T(8,128)S(1)}) custom-call(s32[16]{0:T(128)S(1)} %copy-done.3, f32[1536,128]{1,0:T(8,128)S(1)} %bitcast.7, f32[1536,128]{1,0:T(8,128)S(1)} %collective-permute-done.1.other_ref, f32[1280,128]{1,0:T(8,128)S(1)} %bitcast.10, f32[1280,128]{1,0:T(8,128)S(1)} %collective-permute-done.other_ref.graph_other, ...), custom_call_target="tpu_custom_call" | custom-call | tf_op jit(solution)/shard_map/push_mass/pallas_call | solution.py:687
  75.9 0.2 collective-permute-start.2
  76.1 1.4 %collective-permute-done.2 = f32[512,128]{1,0:T(8,128)S(1)} collective-permute-done((f32[512,128]{1,0:T(8,128)S(1)}, f32[512,128]{1,0:T(8,128)S(1)}, u32[]{:S(2)}, u32[]{:S(2)}) %collective-permute-start.2) | collective-permute-done | bytes 262176 | tf_op jit(solution)/shard_map/ppermute | solution.py:716
  77.5 17.0 %all_to_all.34 = f32[16,32,128]{2,1,0:T(8,128)S(1)} all-to-all(f32[16,32,128]{2,1,0:T(8,128)S(1)} %bitcast.11), channel_id=1, replica_groups=mesh['gx'=4,'gy'=4,'dst'=2] {'gx','gy'}, dimensions={0} | all-to-all | bytes 524288 | tf_op jit(solution)/shard_map/all_to_all | solution.py:712
  94.6 0.1 collective-permute-start.3
  94.7 0.3 multiply_reduce_fusion
  95.0 0.6 broadcast_in_dim.9
  95.6 2.5 %all-to-all-start.3 = ((f32[32,1,32]{2,1,0:T(1,128)}), f32[32,1,32]{2,1,0:T(1,128)S(1)}, u32[]{:S(2)}, u32[]{:S(2)}) async-start(f32[32,1,32]{2,1,0:T(1,128)} %broadcast_in_dim.9), calls=%async_computation.3 | async-start | bytes 32768 | tf_op jit(solution)/shard_map/all_to_all | solution.py:752
  98.2 7.1 %all-to-all-done.3 = f32[32,1,32]{2,1,0:T(1,128)S(1)} async-done(((f32[32,1,32]{2,1,0:T(1,128)}), f32[32,1,32]{2,1,0:T(1,128)S(1)}, u32[]{:S(2)}, u32[]{:S(2)}) %all-to-all-start.3) | async-done | bytes 4128 | tf_op jit(solution)/shard_map/all_to_all | solution.py:752
  105.3 0.5 reduce_sum.29
  105.8 0.0 collective-permute-done.3
  105.8 0.6 sub.6
  (15 shorter events, 0.1 us)
Async XLA Ops:
  3.4 8.5 %copy-start = (s32[8,1024]{1,0:T(8,128)S(1)}, s32[8,1024]{1,0:T(8,128)}, u32[]{:S(2)}) copy-start(s32[8,1024]{1,0:T(8,128)} %valid_any.3) | copy-start | bytes 98308
  3.4 8.5 %copy-start.1 = (s32[8,1024]{1,0:T(8,128)S(1)}, s32[8,1024]{1,0:T(8,128)}, u32[]{:S(2)}) copy-start(s32[8,1024]{1,0:T(8,128)} %succ_any.3) | copy-start | bytes 98308
  3.5 8.5 %copy-start.2 = (s32[4,128]{1,0:T(4,128)S(1)}, s32[4,128]{1,0:T(4,128)}, u32[]{:S(2)}) copy-start(s32[4,128]{1,0:T(4,128)} %border_any.3) | copy-start | bytes 6148
  3.5 8.5 %copy-start.4 = (f32[8,1024]{1,0:T(8,128)S(1)}, f32[8,1024]{1,0:T(8,128)}, u32[]{:S(2)}) copy-start(f32[8,1024]{1,0:T(8,128)} %get-tuple-element.18.reward_ref) | copy-start | bytes 98308
  3.5 27.5 %all-to-all-start.1 = ((f32[16,80,128]{2,1,0:T(8,128)}), f32[16,80,128]{2,1,0:T(8,128)S(1)}, u32[]{:S(2)}, u32[]{:S(2)}) async-start(f32[16,80,128]{2,1,0:T(8,128)} %bitcast.12), calls=%async_computation.1 | async-start | bytes 1310720 | tf_op jit(solution)/shard_map/all_to_all | solution.py:712
  30.9 3.8 %copy-start.5 = (bf16[32,8,1024]{2,1,0:T(8,128)(2,1)S(1)}, bf16[32,8,1024]{2,1,0:T(8,128)(2,1)}, u32[]{:S(2)}) copy-start(bf16[32,8,1024]{2,1,0:T(8,128)(2,1)} %feature_any.1) | copy-start | bytes 1572868
  30.9 25.0 %all-to-all-start = ((f32[16,96,128]{2,1,0:T(8,128)}), f32[16,96,128]{2,1,0:T(8,128)S(1)}, u32[]{:S(2)}, u32[]{:S(2)}) async-start(f32[16,96,128]{2,1,0:T(8,128)} %bitcast), calls=%async_computation | async-start | bytes 1572864 | tf_op jit(solution)/shard_map/all_to_all | solution.py:712
  34.7 2.2 %collective-permute-start = (f32[1280,128]{1,0:T(8,128)S(1)}, f32[1280,128]{1,0:T(8,128)S(1)}, u32[]{:S(2)}, u32[]{:S(2)}) collective-permute-start(f32[1280,128]{1,0:T(8,128)S(1)} %bitcast.8), channel_id=1, source_target_pairs={{0,1},{1,0},{2,3},{3,2},{4,5},{5,4},{6,7},{7,6},{8,9},{9,8},{10,11... | collective-permute-start | bytes 1966088 | tf_op jit(solution)/shard_map/ppermute | solution.py:716
  34.8 0.8 copy-start.6
  35.6 1.3 %copy-start.3 = (s32[16]{0:T(128)S(1)}, s32[16]{0:T(128)}, u32[]{:S(2)}) copy-start(s32[16]{0:T(128)} %dest_ref.3) | copy-start | bytes 196
  55.9 2.3 %collective-permute-start.1 = (f32[1536,128]{1,0:T(8,128)S(1)}, f32[1536,128]{1,0:T(8,128)S(1)}, u32[]{:S(2)}, u32[]{:S(2)}) collective-permute-start(f32[1536,128]{1,0:T(8,128)S(1)} %bitcast.6), channel_id=1, source_target_pairs={{0,1},{1,0},{2,3},{3,2},{4,5},{5,4},{6,7},{7,6},{8,9},{9,8},{10,11... | collective-permute-start | bytes 2359304 | tf_op jit(solution)/shard_map/ppermute | solution.py:716
  75.9 1.6 %collective-permute-start.2 = (f32[512,128]{1,0:T(8,128)S(1)}, f32[512,128]{1,0:T(8,128)S(1)}, u32[]{:S(2)}, u32[]{:S(2)}) collective-permute-start(f32[512,128]{1,0:T(8,128)S(1)} %get-tuple-element.32), channel_id=1, source_target_pairs={{0,1},{1,0},{2,3},{3,2},{4,5},{5,4},{6,7},{7,6},{8,9},{9,8},{10,11... | collective-permute-start | bytes 786440 | tf_op jit(solution)/shard_map/ppermute | solution.py:716
  94.6 11.2 %collective-permute-start.3 = (f32[32,128]{1,0:T(8,128)S(1)}, f32[32,128]{1,0:T(8,128)S(1)}, u32[]{:S(2)}, u32[]{:S(2)}) collective-permute-start(f32[32,128]{1,0:T(8,128)S(1)} %reduce_sum.27), channel_id=1, source_target_pairs={{0,1},{1,0},{2,3},{3,2},{4,5},{5,4},{6,7},{7,6},{8,9},{9,8},{10,11... | collective-permute-start | bytes 49160 | tf_op jit(solution)/shard_map/ppermute | solution.py:716
  95.6 9.6 %all-to-all-start.3 = ((f32[32,1,32]{2,1,0:T(1,128)}), f32[32,1,32]{2,1,0:T(1,128)S(1)}, u32[]{:S(2)}, u32[]{:S(2)}) async-start(f32[32,1,32]{2,1,0:T(1,128)} %broadcast_in_dim.9), calls=%async_computation.3 | async-start | bytes 32768 | tf_op jit(solution)/shard_map/all_to_all | solution.py:752

commit v2 on v1

--- a/solution.py
+++ b/solution.py
@@ -13,9 +13,9 @@
 LANES = 128
 ROWS = 60
 RANKS = -(-ROWS // 16) * 16
-STEP = 19
+STEP = 14
 DEPTH = -(-ROWS // STEP) * STEP
-BLOCK_AXES = ("gx", "gy")
+BLOCK_AXES = ("gy", "gx")
 
 LANE_PICK = lax.GatherDimensionNumbers(
     offset_dims=(),
@@ -82,8 +82,19 @@
     pl.when(jnp.logical_not(first))(lambda: what(other, mine))
 
 
-def own_block(grid_y):
-    return lax.axis_index("gx") * grid_y + lax.axis_index("gy")
+def own_block(grid_x):
+    return lax.axis_index("gy") * grid_x + lax.axis_index("gx")
+
+
+def renumbered(segment, per_block, blocks, grid_x):
+    grid_y = blocks // grid_x
+    block, place = lax.div(segment, per_block), lax.rem(segment, per_block)
+    return (lax.rem(block, grid_y) * grid_x + lax.div(block, grid_y)) * per_block + place
+
+
+def padded_rows(rows):
+    tiles = -(-rows // 8)
+    return (tiles + 1 - tiles % 2) * 8
 
 
 def target_mask(dest, half, chunk, per_block):
@@ -93,12 +104,20 @@
 
 
 def arrange_kernel(
-    succ_any, valid_any, border_any, reward_ref, out_any,
-    succ_ref, valid_ref, border_ref, out_ref, count_ref, first_ref, order_ref, inverse_ref, placed_ref,
+    succ_any, valid_any, border_any, anchor_any, reward_ref, out_any,
+    succ_ref, valid_ref, border_ref, anchor_ref, split_ref, out_ref, count_ref, first_ref, order_ref, inverse_ref, placed_ref,
     pair_ref, lane_ref, code_ref, column_ref, acc_ref, sem
 ):
     run_copies(
-        whole_copies([(succ_any, succ_ref), (valid_any, valid_ref), (border_any, border_ref)], sem)
+        whole_copies(
+            [
+                (succ_any, succ_ref),
+                (valid_any, valid_ref),
+                (border_any, border_ref),
+                (anchor_any, anchor_ref),
+            ],
+            sem,
+        )
     )
     turns, width = succ_ref.shape
     chunks = width // LANES
@@ -239,14 +258,21 @@
             found = jnp.where(listed[:, side : side + 1] == along + q * LANES, down_f + 1.0, 0.0)
             row = share + ROWS + side * chunks + q
             out_ref[row : row + 1, :] = summed_down(found)
+    blocks = anchor_ref.shape[0]
+    for q in range(chunks):
+        split_ref[pl.ds(q, blocks, chunks), :] = anchor_ref[:, q * LANES : (q + 1) * LANES]
     half = out_ref.at[pl.ds(pl.multiple_of(lax.axis_index("dst") * share, 8), share)]
-    blocks = out_any.shape[0] // share
-    run_copies(whole_copies([(half, out_any.at[pl.ds(b * share, share)]) for b in range(blocks)], sem))
+    size = share + chunks
+    pairs = []
+    for b in range(blocks):
+        pairs.append((half, out_any.at[pl.ds(b * size, share)]))
+        pairs.append((split_ref.at[pl.ds(b * chunks, chunks)], out_any.at[pl.ds(b * size + share, chunks)]))
+    run_copies(whole_copies(pairs, sem))
 
 
 def graph_kernel(
-    weight_ref, feature_any, succ_any, valid_any, border_any, anchor_any, out_ref, reward_ref,
-    feature_ref, succ_ref, valid_ref, border_ref, anchor_ref, part_ref, split_ref, sem
+    weight_ref, feature_any, succ_any, valid_any, border_any, out_ref, reward_ref,
+    feature_ref, succ_ref, valid_ref, border_ref, part_ref, sem
 ):
     run_copies(
         whole_copies(
@@ -255,7 +281,6 @@
                 (succ_any, succ_ref),
                 (valid_any, valid_ref),
                 (border_any, border_ref),
-                (anchor_any, anchor_ref),
             ],
             sem,
         )
@@ -275,25 +300,23 @@
         masked = jnp.where(valid_ref[:, cols] == 1, -cost, NEG)
         turn_to = succ_ref[:, cols].astype(jnp.float32)
         part_ref[pl.ds(q, turns, chunks), :] = jnp.where(first_core, masked, turn_to)
-        split_ref[pl.ds(q, anchor_ref.shape[0], chunks), :] = anchor_ref[:, cols]
-    blocks = anchor_ref.shape[0]
-    size, common = out_ref.shape[0] // blocks, part_ref.shape[0]
-    for b in range(blocks):
-        out_ref[b * size : b * size + common, :] = part_ref[...]
-        out_ref[b * size + common : (b + 1) * size, :] = split_ref[b * chunks : (b + 1) * chunks, :]
+    common = part_ref.shape[0]
+    for b in range(out_ref.shape[0] // common):
+        out_ref[b * common : (b + 1) * common, :] = part_ref[...]
 
 
 def value_kernel(
-    grid_y, dest_ref, mine_ref, other_ref, ext_ref, raised_ref, max_ref, inv_ref,
+    grid_x, dest_ref, mine_ref, other_ref, ext_ref, raised_ref, max_ref, inv_ref,
     reward, index, border, side_pad, spare_ref
 ):
     halves = ext_ref.shape[0]
-    size = mine_ref.shape[0] // (8 * halves)
+    blocks = 8 * halves
+    size = mine_ref.shape[0] // blocks
     chunks = ext_ref.shape[1] - 4
     turns = raised_ref.shape[1] // chunks
     edges = turns * chunks
     per_block = chunks * LANES
-    dest = dest_ref[own_block(grid_y)]
+    dest = renumbered(dest_ref[own_block(grid_x)], per_block, blocks, grid_x)
     side_pad[...] = jnp.zeros_like(side_pad)
     sub = lax.broadcasted_iota(jnp.int32, (8, LANES), 0)
     lane = lax.broadcasted_iota(jnp.int32, (8, LANES), 1)
@@ -317,7 +340,7 @@
             found = (border[h, side] == dest_place) & (h * 8 + sub == dest_block)
             entry = jnp.max(jnp.where(found, lane + 1, 0).astype(jnp.float32), axis=1, keepdims=True)
             side_pad[side, 8 + 8 * h : 16 + 8 * h, :] = jnp.broadcast_to(entry, (8, LANES))
-    shifts = ((1, -grid_y), (0, grid_y), (3, -1), (2, 1))
+    shifts = ((1, -1), (0, 1), (3, -grid_x), (2, grid_x))
 
     def shown(h, side):
         facing, by = shifts[side]
@@ -380,7 +403,7 @@
                 store_value(h, q, top, total, into)
             return inner
 
-        lax.fori_loop(0, chunks, one_chunk, 0, unroll=chunks)
+        lax.fori_loop(0, chunks, one_chunk, 0, unroll=chunks // 2)
 
     def two_backups(step, carry):
         backup(spare_ref, ext_ref)
@@ -404,8 +427,8 @@
 
 
 def push_kernel(
-    grid_y, scale, dest_ref, mine_ref, other_ref, graph_mine, graph_other, ext_ref, raised_ref, max_ref,
-    inv_ref, keep_ref, send_ref, ends, order, values, source, slot, policy, back, scaled, total, arrived, side_pad, raw
+    grid_x, scale, dest_ref, mine_ref, other_ref, graph_mine, graph_other, ext_ref, raised_ref, max_ref,
+    inv_ref, keep_ref, send_ref, counts, ends, order, values, source, slot, going, policy, back, scaled, total, arrived, side_pad, raw
 ):
     halves = ext_ref.shape[0]
     blocks = 8 * halves
@@ -415,7 +438,7 @@
     turns = edges // chunks
     per_block = chunks * LANES
     slots = chunks + 4
-    dest = dest_ref[own_block(grid_y)]
+    dest = renumbered(dest_ref[own_block(grid_x)], per_block, blocks, grid_x)
     core = lax.axis_index("dst")
     side_pad[...] = jnp.zeros_like(side_pad)
 
@@ -444,7 +467,7 @@
     deepest = deepest.astype(jnp.int32)
     fits = deepest <= ROWS
     steps = lax.div(jnp.minimum(deepest, ROWS) + (STEP - 1), STEP)
-    shifts = ((1, -grid_y), (0, grid_y), (3, -1), (2, 1))
+    shifts = ((1, -1), (0, 1), (3, -grid_x), (2, grid_x))
 
     def shown(h, side):
         facing, by = shifts[side]
@@ -470,6 +493,7 @@
                 )
 
     def prepare(t, carry):
+        row_before = [None] * halves
         for i in range(STEP):
             for h in range(halves):
                 r = t * STEP + i
@@ -479,6 +503,9 @@
                     jnp.add, [jnp.where(ends[h, n] <= place, 1, 0) for n in range(slots)]
                 )
                 slot[h, r] = row
+                if i:
+                    going[h, r] = jnp.where(row == row_before[h], 1.0, 0.0)
+                row_before[h] = row
                 bits = [(row & (1 << n)) != 0 for n in range(4)]
                 picked = tree_select([values[h, n] for n in range(slots)], bits)
                 top = table_gather([max_ref[h, q] for q in range(chunks)], src)
@@ -488,7 +515,7 @@
     lax.fori_loop(0, steps, prepare, 0)
     for h in range(halves):
         for q in range(chunks):
-            own = of_blocks(graph_mine, h, size - chunks + q, size)
+            own = of_blocks(mine_ref, h, share - chunks + q, share)
             first = jnp.where(target_mask(dest, h, q, per_block), 0.0, own)
             total[h, q] = first
             scaled[h, q] = first * inv_ref[h, q]
@@ -523,13 +550,17 @@
         def one_step(t, carry):
             for h in range(halves):
                 table = [scaled[h, q] for q in range(chunks)]
-                acc = [arrived[h, n] for n in range(slots)]
+                step_sums = [zero] * slots
                 for i in range(STEP):
                     r = t * STEP + i
                     flow = table_gather(table, source[h, r]) * policy[h, r]
-                    acc = add_flow(acc, slot[h, r], flow)
+                    if i:
+                        flow = flow + going[h, r] * so_far
+                    so_far = flow
+                    row = slot[h, r]
+                    step_sums = [jnp.where(row == n, so_far, step_sums[n]) for n in range(slots)]
                 for n in range(slots):
-                    arrived[h, n] = acc[n]
+                    arrived[h, n] = arrived[h, n] + step_sums[n]
             return carry
 
         lax.fori_loop(0, steps, one_step, 0)
@@ -573,14 +604,21 @@
         return carry
 
     lax.fori_loop(0, HORIZON - 1, push, 0)
+    rows_out = edges // 2
+    apart = counts.shape[1] // blocks
     for h in range(halves):
         for q in range(chunks):
             weight = total[h, q] * inv_ref[h, q] * scale
-            for part, out_ref in ((core, keep_ref), (1 - core, send_ref)):
+            for part, piece in ((core, 0), (1 - core, 1)):
                 for a in range(turns // 2):
                     value = weight * raised_ref[h, (part * (turns // 2) + a) * chunks + q]
-                    start = h * 4 * edges + a * chunks + q
-                    out_ref[pl.ds(start, 8, stride=edges // 2), :] = value
+                    start = h * 8 * apart + a * chunks + q
+                    counts[piece, pl.ds(start, 8, stride=apart), :] = value
+    for piece, out_ref in ((0, keep_ref), (1, send_ref)):
+        for b in range(blocks):
+            out_ref[b * rows_out : (b + 1) * rows_out, :] = counts[
+                piece, b * apart : b * apart + rows_out, :
+            ]
 
 
 VMEM_SPEC = pl.BlockSpec(memory_space=pltpu.VMEM)
@@ -593,29 +631,26 @@
     return jax.ShapeDtypeStruct(shape, jnp.float32)
 
 
-def call_graph(cost_weights, features, successors, turn_valid, border_lists, anchors):
+def call_graph(cost_weights, features, successors, turn_valid, border_lists, blocks):
     turns, width = successors.shape
-    blocks = anchors.shape[0]
     chunks = width // LANES
     rows = turns * chunks + 8
     return pl.pallas_call(
         graph_kernel,
-        out_shape=(f32(blocks * (rows + chunks), LANES), f32(turns, width)),
-        in_specs=[SMEM_SPEC] + [HBM_SPEC] * 5,
+        out_shape=(f32(blocks * rows, LANES), f32(turns, width)),
+        in_specs=[SMEM_SPEC] + [HBM_SPEC] * 4,
         out_specs=(VMEM_SPEC, VMEM_SPEC),
         scratch_shapes=[
             pltpu.VMEM(features.shape, features.dtype),
             pltpu.VMEM(successors.shape, jnp.int32),
             pltpu.VMEM(turn_valid.shape, jnp.int32),
             pltpu.VMEM(border_lists.shape, jnp.int32),
-            pltpu.VMEM(anchors.shape, jnp.float32),
             pltpu.VMEM((rows, LANES), jnp.float32),
-            pltpu.VMEM((blocks * chunks, LANES), jnp.float32),
-            pltpu.SemaphoreType.DMA((5,)),
+            pltpu.SemaphoreType.DMA((4,)),
         ],
         compiler_params=pltpu.CompilerParams(vmem_limit_bytes=63 * 1024 * 1024),
         name="own_graph",
-    )(cost_weights, features, successors, turn_valid, border_lists, anchors)
+    )(cost_weights, features, successors, turn_valid, border_lists)
 
 
 def arranged_rows(chunks):
@@ -623,18 +658,21 @@
     return -(-most // 8) * 8
 
 
-def call_arrange(successors, turn_valid, border_lists, reward, blocks):
+def call_arrange(successors, turn_valid, border_lists, anchors, reward):
     chunks = successors.shape[1] // LANES
     share = arranged_rows(chunks)
+    blocks = anchors.shape[0]
     return pl.pallas_call(
         arrange_kernel,
-        out_shape=f32(blocks * share, LANES),
-        in_specs=[HBM_SPEC] * 3 + [VMEM_SPEC],
+        out_shape=f32(blocks * (share + chunks), LANES),
+        in_specs=[HBM_SPEC] * 4 + [VMEM_SPEC],
         out_specs=HBM_SPEC,
         scratch_shapes=[
             pltpu.VMEM(successors.shape, jnp.int32),
             pltpu.VMEM(turn_valid.shape, jnp.int32),
             pltpu.VMEM(border_lists.shape, jnp.int32),
+            pltpu.VMEM(anchors.shape, jnp.float32),
+            pltpu.VMEM((blocks * chunks, LANES), jnp.float32),
             pltpu.VMEM((2 * share, LANES), jnp.float32),
             *[pltpu.VMEM((16, LANES), jnp.float32)] * 5,
             pltpu.VMEM((8, LANES), jnp.float32),
@@ -642,19 +680,19 @@
             pltpu.VMEM(successors.shape, jnp.float32),
             pltpu.VMEM(successors.shape[::-1], jnp.float32),
             pltpu.VMEM((5 * RANKS, LANES), jnp.float32),
-            pltpu.SemaphoreType.DMA((blocks,)),
+            pltpu.SemaphoreType.DMA((2 * blocks,)),
         ],
         compiler_params=PARAMS,
         cost_estimate=pl.CostEstimate(flops=4_000_000_000, bytes_accessed=400_000, transcendentals=0),
         name="arrange_turns",
-    )(successors, turn_valid, border_lists, reward)
-
-
-def call_values(destinations, mine, other, blocks, grid_y, turns, chunks):
+    )(successors, turn_valid, border_lists, anchors, reward)
+
+
+def call_values(destinations, mine, other, blocks, grid_x, turns, chunks):
     halves = blocks // 8
     edges = turns * chunks
     return pl.pallas_call(
-        functools.partial(value_kernel, grid_y),
+        functools.partial(value_kernel, grid_x),
         out_shape=(
             f32(halves, chunks + 4, 8, LANES),
             f32(halves, edges, 8, LANES),
@@ -676,7 +714,7 @@
     )(destinations, mine, other)
 
 
-def call_push(destinations, mine, other, graph_mine, graph_other, ext, raised, top, inv, grid_y, scale):
+def call_push(destinations, mine, other, graph_mine, graph_other, ext, raised, top, inv, grid_x, scale):
     halves, edges = raised.shape[:2]
     blocks = 8 * halves
     chunks = top.shape[1]
@@ -685,16 +723,18 @@
         return pltpu.VMEM((halves, rows, 8, LANES), dtype)
 
     return pl.pallas_call(
-        functools.partial(push_kernel, grid_y, scale),
+        functools.partial(push_kernel, grid_x, scale),
         out_shape=(f32(blocks * edges // 2, LANES),) * 2,
         in_specs=[SMEM_SPEC] + [VMEM_SPEC] * 8,
         out_specs=(VMEM_SPEC,) * 2,
         scratch_shapes=[
+            pltpu.VMEM((2, blocks * padded_rows(edges // 2), LANES), jnp.float32),
             vmem(chunks + 4),
             vmem(chunks + 4, jnp.int32),
             vmem(chunks + 4),
             vmem(DEPTH, jnp.int32),
             vmem(DEPTH, jnp.int32),
+            vmem(DEPTH),
             vmem(DEPTH),
             vmem(4 * chunks, jnp.int32),
             vmem(chunks),
@@ -722,25 +762,25 @@
     turns, own_count = successors.shape
     chunks = own_count // LANES
     edges = turns * chunks
-    grid_y = lax.axis_size("gy")
-    blocks = lax.axis_size("gx") * grid_y
+    grid_x = lax.axis_size("gx")
+    blocks = lax.axis_size("gy") * grid_x
     groups = lax.axis_size("dst")
-    pieces, reward = call_graph(cost_weights, features, successors, turn_valid, border_lists, anchors)
+    pieces, reward = call_graph(cost_weights, features, successors, turn_valid, border_lists, blocks)
     graph = to_blocks(pieces)
-    arranged = call_arrange(successors, turn_valid, border_lists, reward, blocks)
+    arranged = call_arrange(successors, turn_valid, border_lists, anchors, reward)
     core = lax.axis_index("dst")
     demo_term = jnp.where(turn_valid == 1, demo_counts, 0).astype(jnp.float32) / 3.0
     own_feats = lax.dynamic_slice_in_dim(features, core * (turns // 2), turns // 2, axis=1)
     graph = lax.optimization_barrier((graph, arranged))[0]
     arranged = to_blocks(arranged)
     graph = (graph, other_core(graph))
-    values = call_values(destinations, *graph, blocks, grid_y, turns, chunks)
+    values = call_values(destinations, *graph, blocks, grid_x, turns, chunks)
     arranged, own_feats, demo_term, *values = lax.optimization_barrier(
         (arranged, own_feats, demo_term, *values)
     )
     arranged = (arranged, other_core(arranged))
     scale = 1.0 / (anchors.shape[0] * groups * HORIZON)
-    kept, sent = call_push(destinations, *arranged, *graph, *values, grid_y, scale)
+    kept, sent = call_push(destinations, *arranged, *graph, *values, grid_x, scale)
     halved = (kept + other_core(sent)).reshape(blocks, edges // 2, LANES)
     half = jnp.sum(to_blocks(halved), axis=0)
     other = other_core(half)

time: 107 us -> 104 us (0.972)
  waiting for transfers between devices: 20.1 us -> 16.4 us
    all_to_all x2, waiting for transfers between devices: 8.09 us -> 4.53 us  [to_blocks(): return lax.all_to_all(array, BLOCK_AXES, 0, 0, tiled=True)]
  transfers between devices with their start and end apart: 7 -> 7, of which waited for: 6 -> 5; matrix products, arithmetic and copies ran while one was open for 2% -> 2% of each run, Pallas kernels for 28% -> 30%
where the time goes in v2:
time: 104 us
  Pallas kernels  50.6 us (49%)
  blocking collectives  16.8 us (16%)
  waiting for transfers between devices  16.4 us (16%)
  starting transfers between devices  15.9 us (15%)
  other arithmetic  1.57 us (2%)
  local copies, waits for them, and re-layouts  1.43 us (1%)
    pallas_call x1, Pallas kernels, call_values(): pl.pallas_call(functools.partial(value_kernel, grid_x), out_shape=(f32(ha...  19.6 us
    all_to_all x1, blocking collectives, to_blocks(): return lax.all_to_all(array, BLOCK_AXES, 0, 0, tiled=True)  16.8 us
    pallas_call x1, Pallas kernels, call_push(): pl.pallas_call(functools.partial(push_kernel, grid_x, scale), out_shape=(...  16.6 us
    all_to_all x2, starting transfers between devices, to_blocks(): return lax.all_to_all(array, BLOCK_AXES, 0, 0, tiled=True)  12.7 us
    pallas_call x1, Pallas kernels, call_arrange(): pl.pallas_call(arrange_kernel, out_shape=f32(blocks * (share + chunks), L...  11.7 us
    all_to_all x1, waiting for transfers between devices, per_destination(): terms = lax.all_to_all(terms, (*BLOCK_AXES, 'dst'), 0, 0, tiled=True)  7.07 us
    ppermute x4, waiting for transfers between devices, other_core(): return lax.ppermute(array, 'dst', [(0, 1), (1, 0)])  4.84 us
    all_to_all x2, waiting for transfers between devices, to_blocks(): return lax.all_to_all(array, BLOCK_AXES, 0, 0, tiled=True)  4.53 us
  transfers between devices with their start and end apart: 7, of which 5 were waited for; matrix products, arithmetic and copies ran while one was open for 2% of the time, Pallas kernels for 30%

profile of v2, /device:TPU:0, one launch (start us, length us, event | category | flops | bytes accessed | tf_op | source)
XLA Modules:
  0.0 103.6 jit_solution(8590362176468431600)
XLA Ops:
  0.6 2.8 %own_graph.1 = (f32[1152,128]{1,0:T(8,128)}, f32[8,1024]{1,0:T(8,128)}) custom-call(f32[32]{0:T(128)} %weight_ref.1, bf16[32,8,1024]{2,1,0:T(8,128)(2,1)} %feature_any.1, s32[8,1024]{1,0:T(8,128)} %succ_any.3, s32[8,1024]{1,0:T(8,128)} %valid_any.3, s32[4,128]{1,0:T(4,128)} %border_any.3), custom_call_target="tpu_custom_call" | custom-call | tf_op jit(solution)/shard_map/own_graph/pallas_call | solution.py:638
  3.4 0.0 copy-start
  3.4 0.0 copy-start.1
  3.4 0.0 copy-start.2
  3.4 0.0 copy-start.4
  3.4 0.0 copy-start.5
  3.5 8.5 %all-to-all-start.1 = ((f32[16,72,128]{2,1,0:T(8,128)}), f32[16,72,128]{2,1,0:T(8,128)S(1)}, u32[]{:S(2)}, u32[]{:S(2)}) async-start(f32[16,72,128]{2,1,0:T(8,128)} %bitcast.12), calls=%async_computation.1 | async-start | bytes 1179648 | tf_op jit(solution)/shard_map/all_to_all | solution.py:752
  11.9 0.0 copy-done
  12.0 11.7 %arrange_turns.1 = f32[1664,128]{1,0:T(8,128)} custom-call(s32[8,1024]{1,0:T(8,128)S(1)} %copy-done.1, s32[8,1024]{1,0:T(8,128)S(1)} %copy-done, s32[4,128]{1,0:T(4,128)S(1)} %copy-done.2, f32[16,1024]{1,0:T(8,128)S(1)} %copy-done.4, f32[8,1024]{1,0:T(8,128)S(1)} %copy-done.5), custom_call_target="tpu_custom_call" | custom-call | flops 4000000000 | bytes 400000 | tf_op jit(solution)/shard_map/arrange_turns/pallas_call | solution.py:665
  23.7 4.5 %all-to-all-done.1 = f32[16,72,128]{2,1,0:T(8,128)S(1)} async-done(((f32[16,72,128]{2,1,0:T(8,128)}), f32[16,72,128]{2,1,0:T(8,128)S(1)}, u32[]{:S(2)}, u32[]{:S(2)}) %all-to-all-start.1) | async-done | bytes 589856 | tf_op jit(solution)/shard_map/all_to_all | solution.py:752
  28.2 4.3 %all-to-all-start = ((f32[16,104,128]{2,1,0:T(8,128)}), f32[16,104,128]{2,1,0:T(8,128)S(1)}, u32[]{:S(2)}, u32[]{:S(2)}) async-start(f32[16,104,128]{2,1,0:T(8,128)} %bitcast), calls=%async_computation | async-start | bytes 1703936 | tf_op jit(solution)/shard_map/all_to_all | solution.py:752
  32.5 0.1 collective-permute-start
  32.6 0.0 copy-start.7
  32.6 0.1 constant_dynamic-slice_fusion
  32.7 0.6 copy-done.7
  33.4 1.2 %collective-permute-done.other_ref.graph_other = f32[1152,128]{1,0:T(8,128)S(1)} collective-permute-done((f32[1152,128]{1,0:T(8,128)S(1)}, f32[1152,128]{1,0:T(8,128)S(1)}, u32[]{:S(2)}, u32[]{:S(2)}) %collective-permute-start) | collective-permute-done | bytes 589856 | tf_op jit(solution)/shard_map/ppermute | solution.py:756
  34.6 19.6 %soft_values.1 = (f32[2,12,8,128]{3,2,1,0:T(8,128)S(1)}, f32[2,64,8,128]{3,2,1,0:T(8,128)S(1)}, f32[2,8,8,128]{3,2,1,0:T(8,128)S(1)}, f32[2,8,8,128]{3,2,1,0:T(8,128)S(1)}) custom-call(s32[16]{0:T(128)S(1)} %copy-done.3, f32[1152,128]{1,0:T(8,128)S(1)} %bitcast.9, f32[1152,128]{1,0:T(8,128)S(1)} %collective-permute-done.other_ref.graph_other), custom_call_target="tpu_custom_call" | custom-call | flops 40000000 | bytes 40000000 | tf_op jit(solution)/shard_map/soft_values/pallas_call | solution.py:694
  54.2 0.0 all-to-all-done
  54.2 0.2 collective-permute-start.1
  54.4 2.2 %collective-permute-done.1.other_ref = f32[1664,128]{1,0:T(8,128)S(1)} collective-permute-done((f32[1664,128]{1,0:T(8,128)S(1)}, f32[1664,128]{1,0:T(8,128)S(1)}, u32[]{:S(2)}, u32[]{:S(2)}) %collective-permute-start.1) | collective-permute-done | bytes 852000 | tf_op jit(solution)/shard_map/ppermute | solution.py:756
  56.6 16.6 %push_mass.1 = (f32[512,128]{1,0:T(8,128)S(1)}, f32[512,128]{1,0:T(8,128)S(1)}) custom-call(s32[16]{0:T(128)S(1)} %copy-done.3, f32[1664,128]{1,0:T(8,128)S(1)} %bitcast.7, f32[1664,128]{1,0:T(8,128)S(1)} %collective-permute-done.1.other_ref, f32[1152,128]{1,0:T(8,128)S(1)} %bitcast.10, f32[1152,128]{1,0:T(8,128)S(1)} %collective-permute-done.other_ref.graph_other, ...), custom_call_target="tpu_custom_call" | custom-call | tf_op jit(solution)/shard_map/push_mass/pallas_call | solution.py:725
  73.2 0.2 collective-permute-start.2
  73.4 1.4 %collective-permute-done.2 = f32[512,128]{1,0:T(8,128)S(1)} collective-permute-done((f32[512,128]{1,0:T(8,128)S(1)}, f32[512,128]{1,0:T(8,128)S(1)}, u32[]{:S(2)}, u32[]{:S(2)}) %collective-permute-start.2) | collective-permute-done | bytes 262176 | tf_op jit(solution)/shard_map/ppermute | solution.py:756
  74.8 16.8 %all_to_all.34 = f32[16,32,128]{2,1,0:T(8,128)S(1)} all-to-all(f32[16,32,128]{2,1,0:T(8,128)S(1)} %bitcast.11), channel_id=1, replica_groups=mesh['gx'=4,'gy'=4,'dst'=2] {'gy','gx'}, dimensions={0} | all-to-all | bytes 524288 | tf_op jit(solution)/shard_map/all_to_all | solution.py:752
  91.7 0.1 collective-permute-start.3
  91.8 0.3 multiply_reduce_fusion
  92.1 0.6 broadcast_in_dim.9
  92.7 2.6 %all-to-all-start.3 = ((f32[32,1,32]{2,1,0:T(1,128)}), f32[32,1,32]{2,1,0:T(1,128)S(1)}, u32[]{:S(2)}, u32[]{:S(2)}) async-start(f32[32,1,32]{2,1,0:T(1,128)} %broadcast_in_dim.9), calls=%async_computation.3 | async-start | bytes 32768 | tf_op jit(solution)/shard_map/all_to_all | solution.py:792
  95.4 7.1 %all-to-all-done.3 = f32[32,1,32]{2,1,0:T(1,128)S(1)} async-done(((f32[32,1,32]{2,1,0:T(1,128)}), f32[32,1,32]{2,1,0:T(1,128)S(1)}, u32[]{:S(2)}, u32[]{:S(2)}) %all-to-all-start.3) | async-done | bytes 4128 | tf_op jit(solution)/shard_map/all_to_all | solution.py:792
  102.4 0.5 reduce_sum.29
  103.0 0.0 collective-permute-done.3
  103.0 0.6 sub.6
  (17 shorter events, 0.1 us)
Async XLA Ops:
  3.4 8.5 %copy-start = (s32[8,1024]{1,0:T(8,128)S(1)}, s32[8,1024]{1,0:T(8,128)}, u32[]{:S(2)}) copy-start(s32[8,1024]{1,0:T(8,128)} %valid_any.3) | copy-start | bytes 98308
  3.4 8.5 %copy-start.1 = (s32[8,1024]{1,0:T(8,128)S(1)}, s32[8,1024]{1,0:T(8,128)}, u32[]{:S(2)}) copy-start(s32[8,1024]{1,0:T(8,128)} %succ_any.3) | copy-start | bytes 98308
  3.4 8.5 %copy-start.2 = (s32[4,128]{1,0:T(4,128)S(1)}, s32[4,128]{1,0:T(4,128)}, u32[]{:S(2)}) copy-start(s32[4,128]{1,0:T(4,128)} %border_any.3) | copy-start | bytes 6148
  3.4 8.5 %copy-start.4 = (f32[16,1024]{1,0:T(8,128)S(1)}, f32[16,1024]{1,0:T(8,128)}, u32[]{:S(2)}) copy-start(f32[16,1024]{1,0:T(8,128)} %anchor_any.1) | copy-start | bytes 196612
  3.4 8.5 %copy-start.5 = (f32[8,1024]{1,0:T(8,128)S(1)}, f32[8,1024]{1,0:T(8,128)}, u32[]{:S(2)}) copy-start(f32[8,1024]{1,0:T(8,128)} %get-tuple-element.18.reward_ref) | copy-start | bytes 98308
  3.5 24.7 %all-to-all-start.1 = ((f32[16,72,128]{2,1,0:T(8,128)}), f32[16,72,128]{2,1,0:T(8,128)S(1)}, u32[]{:S(2)}, u32[]{:S(2)}) async-start(f32[16,72,128]{2,1,0:T(8,128)} %bitcast.12), calls=%async_computation.1 | async-start | bytes 1179648 | tf_op jit(solution)/shard_map/all_to_all | solution.py:752
  28.2 4.4 %copy-start.6 = (bf16[32,8,1024]{2,1,0:T(8,128)(2,1)S(1)}, bf16[32,8,1024]{2,1,0:T(8,128)(2,1)}, u32[]{:S(2)}) copy-start(bf16[32,8,1024]{2,1,0:T(8,128)(2,1)} %feature_any.1) | copy-start | bytes 1572868
  28.2 26.0 %all-to-all-start = ((f32[16,104,128]{2,1,0:T(8,128)}), f32[16,104,128]{2,1,0:T(8,128)S(1)}, u32[]{:S(2)}, u32[]{:S(2)}) async-start(f32[16,104,128]{2,1,0:T(8,128)} %bitcast), calls=%async_computation | async-start | bytes 1703936 | tf_op jit(solution)/shard_map/all_to_all | solution.py:752
  32.5 2.1 %collective-permute-start = (f32[1152,128]{1,0:T(8,128)S(1)}, f32[1152,128]{1,0:T(8,128)S(1)}, u32[]{:S(2)}, u32[]{:S(2)}) collective-permute-start(f32[1152,128]{1,0:T(8,128)S(1)} %bitcast.8), channel_id=1, source_target_pairs={{0,1},{1,0},{2,3},{3,2},{4,5},{5,4},{6,7},{7,6},{8,9},{9,8},{10,11... | collective-permute-start | bytes 1769480 | tf_op jit(solution)/shard_map/ppermute | solution.py:756
  32.6 0.8 copy-start.7
  33.3 1.2 %copy-start.3 = (s32[16]{0:T(128)S(1)}, s32[16]{0:T(128)}, u32[]{:S(2)}) copy-start(s32[16]{0:T(128)} %dest_ref.3) | copy-start | bytes 196
  54.2 2.4 %collective-permute-start.1 = (f32[1664,128]{1,0:T(8,128)S(1)}, f32[1664,128]{1,0:T(8,128)S(1)}, u32[]{:S(2)}, u32[]{:S(2)}) collective-permute-start(f32[1664,128]{1,0:T(8,128)S(1)} %bitcast.6), channel_id=1, source_target_pairs={{0,1},{1,0},{2,3},{3,2},{4,5},{5,4},{6,7},{7,6},{8,9},{9,8},{10,11... | collective-permute-start | bytes 2555912 | tf_op jit(solution)/shard_map/ppermute | solution.py:756
  73.2 1.6 %collective-permute-start.2 = (f32[512,128]{1,0:T(8,128)S(1)}, f32[512,128]{1,0:T(8,128)S(1)}, u32[]{:S(2)}, u32[]{:S(2)}) collective-permute-start(f32[512,128]{1,0:T(8,128)S(1)} %get-tuple-element.32), channel_id=1, source_target_pairs={{0,1},{1,0},{2,3},{3,2},{4,5},{5,4},{6,7},{7,6},{8,9},{9,8},{10,11... | collective-permute-start | bytes 786440 | tf_op jit(solution)/shard_map/ppermute | solution.py:756
  91.7 11.3 %collective-permute-start.3 = (f32[32,128]{1,0:T(8,128)S(1)}, f32[32,128]{1,0:T(8,128)S(1)}, u32[]{:S(2)}, u32[]{:S(2)}) collective-permute-start(f32[32,128]{1,0:T(8,128)S(1)} %reduce_sum.27), channel_id=1, source_target_pairs={{0,1},{1,0},{2,3},{3,2},{4,5},{5,4},{6,7},{7,6},{8,9},{9,8},{10,11... | collective-permute-start | bytes 49160 | tf_op jit(solution)/shard_map/ppermute | solution.py:756
  92.7 9.7 %all-to-all-start.3 = ((f32[32,1,32]{2,1,0:T(1,128)}), f32[32,1,32]{2,1,0:T(1,128)S(1)}, u32[]{:S(2)}, u32[]{:S(2)}) async-start(f32[32,1,32]{2,1,0:T(1,128)} %broadcast_in_dim.9), calls=%async_computation.3 | async-start | bytes 32768 | tf_op jit(solution)/shard_map/all_to_all | solution.py:792

commit v3 on v2

--- a/solution.py
+++ b/solution.py
@@ -305,13 +305,24 @@
         out_ref[b * common : (b + 1) * common, :] = part_ref[...]
 
 
+def regroup_kernel(pieces_ref, out_ref):
+    halves, rows = out_ref.shape[:2]
+    size = pieces_ref.shape[0] // (8 * halves)
+    for h in range(halves):
+
+        def one_row(i, carry, h=h):
+            out_ref[h, i] = of_blocks(pieces_ref, h, i, size)
+            return carry
+
+        lax.fori_loop(0, rows, one_row, 0, unroll=8)
+
+
 def value_kernel(
     grid_x, dest_ref, mine_ref, other_ref, ext_ref, raised_ref, max_ref, inv_ref,
     reward, index, border, side_pad, spare_ref
 ):
     halves = ext_ref.shape[0]
     blocks = 8 * halves
-    size = mine_ref.shape[0] // blocks
     chunks = ext_ref.shape[1] - 4
     turns = raised_ref.shape[1] // chunks
     edges = turns * chunks
@@ -326,13 +337,13 @@
         for h in range(halves):
 
             def rows(i, carry, h=h):
-                reward[h, i] = of_blocks(first, h, i, size)
-                index[h, i] = of_blocks(second, h, i, size).astype(jnp.int32)
+                reward[h, i] = first[h, i]
+                index[h, i] = second[h, i].astype(jnp.int32)
                 return carry
 
             lax.fori_loop(0, edges, rows, 0, unroll=8)
             for side in range(4):
-                border[h, side] = of_blocks(first, h, edges + side, size).astype(jnp.int32)
+                border[h, side] = first[h, edges + side].astype(jnp.int32)
 
     by_core(unpack, mine_ref, other_ref)
     for h in range(halves):
@@ -403,7 +414,7 @@
                 store_value(h, q, top, total, into)
             return inner
 
-        lax.fori_loop(0, chunks, one_chunk, 0, unroll=chunks // 2)
+        lax.fori_loop(0, chunks, one_chunk, 0, unroll=chunks)
 
     def two_backups(step, carry):
         backup(spare_ref, ext_ref)
@@ -432,7 +443,7 @@
 ):
     halves = ext_ref.shape[0]
     blocks = 8 * halves
-    size, share = graph_mine.shape[0] // blocks, mine_ref.shape[0] // blocks
+    share = mine_ref.shape[1]
     chunks = max_ref.shape[1]
     edges = raised_ref.shape[1]
     turns = edges // chunks
@@ -445,14 +456,14 @@
     def unpack(first, second):
         for h in range(halves):
             for n in range(slots):
-                ends[h, n] = of_blocks(first, h, ROWS + n, share)
-                order[h, n] = of_blocks(first, h, ROWS + slots + n, share).astype(jnp.int32)
-                inverse = of_blocks(first, h, ROWS + 2 * slots + n, share).astype(jnp.int32)
+                ends[h, n] = first[h, ROWS + n]
+                order[h, n] = first[h, ROWS + slots + n].astype(jnp.int32)
+                inverse = first[h, ROWS + 2 * slots + n].astype(jnp.int32)
                 values[h, n] = lane_gather(ext_ref[h, n], inverse)
 
             def rows(r, carry, h=h):
-                source[h, r] = of_blocks(first, h, r, share).astype(jnp.int32)
-                policy[h, r] = of_blocks(second, h, r, share)
+                source[h, r] = first[h, r].astype(jnp.int32)
+                policy[h, r] = second[h, r]
                 return carry
 
             lax.fori_loop(0, ROWS, rows, 0, unroll=6)
@@ -460,7 +471,7 @@
                 source[h, r] = jnp.zeros((8, LANES), jnp.int32)
                 policy[h, r] = jnp.zeros((8, LANES), jnp.float32)
             for n in range(4 * chunks):
-                back[h, n] = of_blocks(second, h, ROWS + n, share).astype(jnp.int32) - 1
+                back[h, n] = second[h, ROWS + n].astype(jnp.int32) - 1
 
     by_core(unpack, mine_ref, other_ref)
     deepest = jnp.max(functools.reduce(jnp.maximum, [ends[h, slots - 1] for h in range(halves)]))
@@ -515,7 +526,7 @@
     lax.fori_loop(0, steps, prepare, 0)
     for h in range(halves):
         for q in range(chunks):
-            own = of_blocks(mine_ref, h, share - chunks + q, share)
+            own = mine_ref[h, share - chunks + q]
             first = jnp.where(target_mask(dest, h, q, per_block), 0.0, own)
             total[h, q] = first
             scaled[h, q] = first * inv_ref[h, q]
@@ -526,7 +537,7 @@
             for h in range(halves):
 
                 def rows(e, carry, h=h):
-                    raw[h, e] = of_blocks(second, h, e, size).astype(jnp.int32)
+                    raw[h, e] = second[h, e].astype(jnp.int32)
                     return carry
 
                 lax.fori_loop(0, edges, rows, 0)
@@ -688,6 +699,17 @@
     )(successors, turn_valid, border_lists, anchors, reward)
 
 
+def call_regroup(pieces, blocks):
+    return pl.pallas_call(
+        regroup_kernel,
+        out_shape=f32(blocks // 8, pieces.shape[0] // blocks, 8, LANES),
+        in_specs=[VMEM_SPEC],
+        out_specs=VMEM_SPEC,
+        compiler_params=PARAMS,
+        name="regroup",
+    )(pieces)
+
+
 def call_values(destinations, mine, other, blocks, grid_x, turns, chunks):
     halves = blocks // 8
     edges = turns * chunks
@@ -773,11 +795,13 @@
     own_feats = lax.dynamic_slice_in_dim(features, core * (turns // 2), turns // 2, axis=1)
     graph = lax.optimization_barrier((graph, arranged))[0]
     arranged = to_blocks(arranged)
+    graph = call_regroup(graph, blocks)
     graph = (graph, other_core(graph))
     values = call_values(destinations, *graph, blocks, grid_x, turns, chunks)
     arranged, own_feats, demo_term, *values = lax.optimization_barrier(
         (arranged, own_feats, demo_term, *values)
     )
+    arranged = call_regroup(arranged, blocks)
     arranged = (arranged, other_core(arranged))
     scale = 1.0 / (anchors.shape[0] * groups * HORIZON)
     kept, sent = call_push(destinations, *arranged, *graph, *values, grid_x, scale)

time: 104 us -> 103 us (level)
    pallas_call x1, Pallas kernels: 19.6 us -> 18.2 us  [call_values(): pl.pallas_call(functools.partial(value_kernel, grid_x), out_shape=(f32(ha...]
  transfers between devices with their start and end apart: 7 -> 7, of which waited for: 5 -> 5; matrix products, arithmetic and copies ran while one was open for 2% -> 2% of each run, Pallas kernels for 30% -> 29%
where the time goes in v3:
time: 103 us
  Pallas kernels  49.7 us (48%)
  blocking collectives  16.9 us (16%)
  waiting for transfers between devices  15.8 us (15%)
  starting transfers between devices  15.7 us (15%)
  local copies, waits for them, and re-layouts  2.44 us (2%)
  other arithmetic  1.57 us (2%)
    pallas_call x1, Pallas kernels, call_values(): pl.pallas_call(functools.partial(value_kernel, grid_x), out_shape=(f32(ha...  18.2 us
    all_to_all x1, blocking collectives, to_blocks(): return lax.all_to_all(array, BLOCK_AXES, 0, 0, tiled=True)  16.9 us
    pallas_call x1, Pallas kernels, call_push(): pl.pallas_call(functools.partial(push_kernel, grid_x, scale), out_shape=(...  16.6 us
    all_to_all x2, starting transfers between devices, to_blocks(): return lax.all_to_all(array, BLOCK_AXES, 0, 0, tiled=True)  12.6 us
    pallas_call x1, Pallas kernels, call_arrange(): pl.pallas_call(arrange_kernel, out_shape=f32(blocks * (share + chunks), L...  11.7 us
    all_to_all x1, waiting for transfers between devices, per_destination(): terms = lax.all_to_all(terms, (*BLOCK_AXES, 'dst'), 0, 0, tiled=True)  7.07 us
    all_to_all x2, waiting for transfers between devices, to_blocks(): return lax.all_to_all(array, BLOCK_AXES, 0, 0, tiled=True)  4.52 us
    ppermute x4, waiting for transfers between devices, other_core(): return lax.ppermute(array, 'dst', [(0, 1), (1, 0)])  4.18 us
  transfers between devices with their start and end apart: 7, of which 5 were waited for; matrix products, arithmetic and copies ran while one was open for 2% of the time, Pallas kernels for 29%

profile of v3, /device:TPU:0, one launch (start us, length us, event | category | flops | bytes accessed | tf_op | source)
XLA Modules:
  0.0 102.9 jit_solution(2494611501593467682)
XLA Ops:
  0.6 2.8 %own_graph.1 = (f32[1152,128]{1,0:T(8,128)}, f32[8,1024]{1,0:T(8,128)}) custom-call(f32[32]{0:T(128)} %weight_ref.1, bf16[32,8,1024]{2,1,0:T(8,128)(2,1)} %feature_any.1, s32[8,1024]{1,0:T(8,128)} %succ_any.3, s32[8,1024]{1,0:T(8,128)} %valid_any.3, s32[4,128]{1,0:T(4,128)} %border_any.3), custom_call_target="tpu_custom_call" | custom-call | tf_op jit(solution)/shard_map/own_graph/pallas_call | solution.py:649
  3.4 0.0 copy-start
  3.4 0.0 copy-start.1
  3.4 0.0 copy-start.2
  3.4 0.0 copy-start.4
  3.4 0.0 copy-start.5
  3.5 8.5 %all-to-all-start.1 = ((f32[16,72,128]{2,1,0:T(8,128)}), f32[16,72,128]{2,1,0:T(8,128)S(1)}, u32[]{:S(2)}, u32[]{:S(2)}) async-start(f32[16,72,128]{2,1,0:T(8,128)} %bitcast.9), calls=%async_computation.1 | async-start | bytes 1179648 | tf_op jit(solution)/shard_map/all_to_all | solution.py:774
  12.0 11.7 %arrange_turns.1 = f32[1664,128]{1,0:T(8,128)} custom-call(s32[8,1024]{1,0:T(8,128)S(1)} %copy-done.1, s32[8,1024]{1,0:T(8,128)S(1)} %copy-done, s32[4,128]{1,0:T(4,128)S(1)} %copy-done.2, f32[16,1024]{1,0:T(8,128)S(1)} %copy-done.4, f32[8,1024]{1,0:T(8,128)S(1)} %copy-done.5), custom_call_target="tpu_custom_call" | custom-call | flops 4000000000 | bytes 400000 | tf_op jit(solution)/shard_map/arrange_turns/pallas_call | solution.py:676
  23.7 4.5 %all-to-all-done.1 = f32[16,72,128]{2,1,0:T(8,128)S(1)} async-done(((f32[16,72,128]{2,1,0:T(8,128)}), f32[16,72,128]{2,1,0:T(8,128)S(1)}, u32[]{:S(2)}, u32[]{:S(2)}) %all-to-all-start.1) | async-done | bytes 589856 | tf_op jit(solution)/shard_map/all_to_all | solution.py:774
  28.2 4.2 %all-to-all-start = ((f32[16,104,128]{2,1,0:T(8,128)}), f32[16,104,128]{2,1,0:T(8,128)S(1)}, u32[]{:S(2)}, u32[]{:S(2)}) async-start(f32[16,104,128]{2,1,0:T(8,128)} %bitcast), calls=%async_computation | async-start | bytes 1703936 | tf_op jit(solution)/shard_map/all_to_all | solution.py:774
  32.4 0.2 regroup.2.mine_ref.graph_mine
  32.5 0.1 collective-permute-start
  32.6 0.8 copy-done.6
  33.4 0.1 constant_dynamic-slice_fusion
  33.5 0.6 copy-done.7
  34.2 0.4 collective-permute-done.other_ref.graph_other
  34.6 0.2 copy-done.3
  34.8 18.2 %soft_values.1 = (f32[2,12,8,128]{3,2,1,0:T(8,128)S(1)}, f32[2,64,8,128]{3,2,1,0:T(8,128)S(1)}, f32[2,8,8,128]{3,2,1,0:T(8,128)S(1)}, f32[2,8,8,128]{3,2,1,0:T(8,128)S(1)}) custom-call(s32[16]{0:T(128)S(1)} %copy-done.3, f32[2,72,8,128]{3,2,1,0:T(8,128)S(1)} %regroup.2.mine_ref.graph_mine, f32[2,72,8,128]{3,2,1,0:T(8,128)S(1)} %collective-permute-done.other_ref.graph_other), custom_call_target="tpu_custom_call" | custom-call | flops 40000000 | bytes 40000000 | tf_op jit(solution)/shard_map/soft_values/pallas_call | solution.py:716
  53.0 0.2 regroup.3.mine_ref
  53.3 0.1 collective-permute-start.1
  53.3 2.4 %collective-permute-done.1.other_ref = f32[2,104,8,128]{3,2,1,0:T(8,128)S(1)} collective-permute-done((f32[2,104,8,128]{3,2,1,0:T(8,128)S(1)}, f32[2,104,8,128]{3,2,1,0:T(8,128)S(1)}, u32[]{:S(2)}, u32[]{:S(2)}) %collective-permute-start.1) | collective-permute-done | bytes 852000 | tf_op jit(solution)/shard_map/ppermute | solution.py:778
  55.7 16.6 %push_mass.1 = (f32[512,128]{1,0:T(8,128)S(1)}, f32[512,128]{1,0:T(8,128)S(1)}) custom-call(s32[16]{0:T(128)S(1)} %copy-done.3, f32[2,104,8,128]{3,2,1,0:T(8,128)S(1)} %regroup.3.mine_ref, f32[2,104,8,128]{3,2,1,0:T(8,128)S(1)} %collective-permute-done.1.other_ref, f32[2,72,8,128]{3,2,1,0:T(8,128)S(1)} %regroup.2.mine_ref.graph_mine, ...), custom_call_target="tpu_custom_call" | custom-call | tf_op jit(solution)/shard_map/push_mass/pallas_call | solution.py:747
  72.3 0.2 collective-permute-start.2
  72.6 1.4 %collective-permute-done.2 = f32[512,128]{1,0:T(8,128)S(1)} collective-permute-done((f32[512,128]{1,0:T(8,128)S(1)}, f32[512,128]{1,0:T(8,128)S(1)}, u32[]{:S(2)}, u32[]{:S(2)}) %collective-permute-start.2) | collective-permute-done | bytes 262176 | tf_op jit(solution)/shard_map/ppermute | solution.py:778
  74.0 16.9 %all_to_all.34 = f32[16,32,128]{2,1,0:T(8,128)S(1)} all-to-all(f32[16,32,128]{2,1,0:T(8,128)S(1)} %bitcast.8), channel_id=1, replica_groups=mesh['gx'=4,'gy'=4,'dst'=2] {'gy','gx'}, dimensions={0} | all-to-all | bytes 524288 | tf_op jit(solution)/shard_map/all_to_all | solution.py:774
  90.9 0.1 collective-permute-start.3
  91.0 0.3 multiply_reduce_fusion
  91.3 0.6 broadcast_in_dim.9
  92.0 2.6 %all-to-all-start.3 = ((f32[32,1,32]{2,1,0:T(1,128)}), f32[32,1,32]{2,1,0:T(1,128)S(1)}, u32[]{:S(2)}, u32[]{:S(2)}) async-start(f32[32,1,32]{2,1,0:T(1,128)} %broadcast_in_dim.9), calls=%async_computation.3 | async-start | bytes 32768 | tf_op jit(solution)/shard_map/all_to_all | solution.py:816
  94.6 7.1 %all-to-all-done.3 = f32[32,1,32]{2,1,0:T(1,128)S(1)} async-done(((f32[32,1,32]{2,1,0:T(1,128)}), f32[32,1,32]{2,1,0:T(1,128)S(1)}, u32[]{:S(2)}, u32[]{:S(2)}) %all-to-all-start.3) | async-done | bytes 4128 | tf_op jit(solution)/shard_map/all_to_all | solution.py:816
  101.7 0.5 reduce_sum.29
  102.2 0.6 sub.6
  (19 shorter events, 0.1 us)
Async XLA Ops:
  3.4 8.5 %copy-start = (s32[8,1024]{1,0:T(8,128)S(1)}, s32[8,1024]{1,0:T(8,128)}, u32[]{:S(2)}) copy-start(s32[8,1024]{1,0:T(8,128)} %valid_any.3) | copy-start | bytes 98308
  3.4 8.5 %copy-start.1 = (s32[8,1024]{1,0:T(8,128)S(1)}, s32[8,1024]{1,0:T(8,128)}, u32[]{:S(2)}) copy-start(s32[8,1024]{1,0:T(8,128)} %succ_any.3) | copy-start | bytes 98308
  3.4 8.5 %copy-start.2 = (s32[4,128]{1,0:T(4,128)S(1)}, s32[4,128]{1,0:T(4,128)}, u32[]{:S(2)}) copy-start(s32[4,128]{1,0:T(4,128)} %border_any.3) | copy-start | bytes 6148
  3.4 8.5 %copy-start.4 = (f32[16,1024]{1,0:T(8,128)S(1)}, f32[16,1024]{1,0:T(8,128)}, u32[]{:S(2)}) copy-start(f32[16,1024]{1,0:T(8,128)} %anchor_any.1) | copy-start | bytes 196612
  3.4 8.5 %copy-start.5 = (f32[8,1024]{1,0:T(8,128)S(1)}, f32[8,1024]{1,0:T(8,128)}, u32[]{:S(2)}) copy-start(f32[8,1024]{1,0:T(8,128)} %get-tuple-element.18.reward_ref) | copy-start | bytes 98308
  3.5 24.7 %all-to-all-start.1 = ((f32[16,72,128]{2,1,0:T(8,128)}), f32[16,72,128]{2,1,0:T(8,128)S(1)}, u32[]{:S(2)}, u32[]{:S(2)}) async-start(f32[16,72,128]{2,1,0:T(8,128)} %bitcast.9), calls=%async_computation.1 | async-start | bytes 1179648 | tf_op jit(solution)/shard_map/all_to_all | solution.py:774
  28.2 24.8 %all-to-all-start = ((f32[16,104,128]{2,1,0:T(8,128)}), f32[16,104,128]{2,1,0:T(8,128)S(1)}, u32[]{:S(2)}, u32[]{:S(2)}) async-start(f32[16,104,128]{2,1,0:T(8,128)} %bitcast), calls=%async_computation | async-start | bytes 1703936 | tf_op jit(solution)/shard_map/all_to_all | solution.py:774
  32.4 1.0 %copy-start.6 = (bf16[32,8,1024]{2,1,0:T(8,128)(2,1)S(1)}, bf16[32,8,1024]{2,1,0:T(8,128)(2,1)}, u32[]{:S(2)}) copy-start(bf16[32,8,1024]{2,1,0:T(8,128)(2,1)} %feature_any.1) | copy-start | bytes 1572868
  32.5 2.1 %collective-permute-start = (f32[2,72,8,128]{3,2,1,0:T(8,128)S(1)}, f32[2,72,8,128]{3,2,1,0:T(8,128)S(1)}, u32[]{:S(2)}, u32[]{:S(2)}) collective-permute-start(f32[2,72,8,128]{3,2,1,0:T(8,128)S(1)} %regroup.2.mine_ref.graph_mine), channel_id=1, source_target_pairs={{0,1},{1,0},{2,3},{3,2},{4,5},{5,4},{6,7},{7,6},{8,9},{9,8},{10,11... | collective-permute-start | bytes 1769480 | tf_op jit(solution)/shard_map/ppermute | solution.py:778
  33.4 0.8 copy-start.7
  34.2 0.7 copy-start.3
  53.3 2.4 %collective-permute-start.1 = (f32[2,104,8,128]{3,2,1,0:T(8,128)S(1)}, f32[2,104,8,128]{3,2,1,0:T(8,128)S(1)}, u32[]{:S(2)}, u32[]{:S(2)}) collective-permute-start(f32[2,104,8,128]{3,2,1,0:T(8,128)S(1)} %regroup.3.mine_ref), channel_id=1, source_target_pairs={{0,1},{1,0},{2,3},{3,2},{4,5},{5,4},{6,7},{7,6},{8,9},{9,8},{10,11... | collective-permute-start | bytes 2555912 | tf_op jit(solution)/shard_map/ppermute | solution.py:778
  72.3 1.6 %collective-permute-start.2 = (f32[512,128]{1,0:T(8,128)S(1)}, f32[512,128]{1,0:T(8,128)S(1)}, u32[]{:S(2)}, u32[]{:S(2)}) collective-permute-start(f32[512,128]{1,0:T(8,128)S(1)} %get-tuple-element.32), channel_id=1, source_target_pairs={{0,1},{1,0},{2,3},{3,2},{4,5},{5,4},{6,7},{7,6},{8,9},{9,8},{10,11... | collective-permute-start | bytes 786440 | tf_op jit(solution)/shard_map/ppermute | solution.py:778
  90.9 11.3 %collective-permute-start.3 = (f32[32,128]{1,0:T(8,128)S(1)}, f32[32,128]{1,0:T(8,128)S(1)}, u32[]{:S(2)}, u32[]{:S(2)}) collective-permute-start(f32[32,128]{1,0:T(8,128)S(1)} %reduce_sum.27), channel_id=1, source_target_pairs={{0,1},{1,0},{2,3},{3,2},{4,5},{5,4},{6,7},{7,6},{8,9},{9,8},{10,11... | collective-permute-start | bytes 49160 | tf_op jit(solution)/shard_map/ppermute | solution.py:778
  92.0 9.7 %all-to-all-start.3 = ((f32[32,1,32]{2,1,0:T(1,128)}), f32[32,1,32]{2,1,0:T(1,128)S(1)}, u32[]{:S(2)}, u32[]{:S(2)}) async-start(f32[32,1,32]{2,1,0:T(1,128)} %broadcast_in_dim.9), calls=%async_computation.3 | async-start | bytes 32768 | tf_op jit(solution)/shard_map/all_to_all | solution.py:816
